TPU v7x, 256 devices: a whole 4x4x8 slice. The times are simulated.
256 devices in a mesh: dp: 128 (over y, x, z_lo, core), tensor: 2 (over z_hi).
Axes of the slice: x: 4, y: 4, z: 8 (z_hi: 2, z_lo: 4; z = z_hi * 4 + z_lo), core: 2. Of those that a mesh axis runs over, the one named last changes fastest.
Arguments:
- x_in: bfloat16 [32768, 768], P('dp'), may hold values from -6 to 6
- lengths: int32 [128], P('dp'), may hold values from 51 to 256, as said below
- retrieved: int32 [32768, 1024], P('dp'), may hold values from 0 to 8191, all different within a row
- datastore: bfloat16 [8192, 768], P('dp'), may hold values from -6 to 6
- self_wq: bfloat16 [768, 768], P(None, 'tensor'), may hold values from -0.21875 to 0.21875
- self_wk: bfloat16 [768, 768], P(None, 'tensor'), may hold values from -0.21875 to 0.21875
- self_wv: bfloat16 [768, 768], P(None, 'tensor'), may hold values from -0.21875 to 0.21875
- self_wo: bfloat16 [768, 768], P('tensor'), may hold values from -1.75 to 1.75
- ln1_gain: float32 [768], replicated, may hold values from 0.1 to 1.9
- ln1_bias: float32 [768], replicated, may hold values from -3 to 3
- cross_wq: bfloat16 [768, 768], P(None, 'tensor'), may hold values from -0.3125 to 0.3125
- cross_wk: bfloat16 [768, 768], P(None, 'tensor'), may hold values from -0.21875 to 0.21875
- cross_wv: bfloat16 [768, 768], P(None, 'tensor'), may hold values from -0.21875 to 0.21875
- cross_wo: bfloat16 [768, 768], P('tensor'), may hold values from -2.5 to 2.5
- ln2_gain: float32 [768], replicated, may hold values from 0.1 to 1.9
- ln2_bias: float32 [768], replicated, may hold values from -3 to 3
- ffn_w1: bfloat16 [768, 3072], P(None, 'tensor'), may hold values from -0.21875 to 0.21875
- ffn_w2: bfloat16 [3072, 768], P('tensor'), may hold values from -0.109375 to 0.109375
- ln3_gain: float32 [768], replicated, may hold values from 0.1 to 1.9
- ln3_bias: float32 [768], replicated, may hold values from -3 to 3
- cotangent: bfloat16 [32768, 768], P('dp'), may hold values from -6 to 6
Outputs:
- block_out: bfloat16 [32768, 768], P('dp')
- input_grad: float32 [32768, 768], P('dp')
- datastore_grad: float32 [8192, 768], P('dp', 'tensor')
- self_wq_grad: float32 [768, 768], P('dp', 'tensor')
- self_wk_grad: float32 [768, 768], P('dp', 'tensor')
- self_wv_grad: float32 [768, 768], P('dp', 'tensor')
- self_wo_grad: float32 [768, 768], P('tensor', 'dp')
- ln1_gain_grad: float32 [768], P('dp')
- ln1_bias_grad: float32 [768], P('dp')
- cross_wq_grad: float32 [768, 768], P('dp', 'tensor')
- cross_wk_grad: float32 [768, 768], P('dp', 'tensor')
- cross_wv_grad: float32 [768, 768], P('dp', 'tensor')
- cross_wo_grad: float32 [768, 768], P('tensor', 'dp')
- ln2_gain_grad: float32 [768], P('dp')
- ln2_bias_grad: float32 [768], P('dp')
- ffn_w1_grad: float32 [768, 3072], P('dp', 'tensor')
- ffn_w2_grad: float32 [3072, 768], P('tensor', 'dp')
- ln3_gain_grad: float32 [768], P('dp')
- ln3_bias_grad: float32 [768], P('dp')
Inputs may be any that keep to these rules, and one draw needn't show every extreme that they name: `lengths`: one sequence in every draw has all 256 slots valid. `retrieved`: each row names 1024 different datastore states.
All inputs are finite; a program needn't handle non-finite values.
Results may differ from a plain program's by a relative error of at most 0.033.
Values may be sent and summed in bfloat16 or wider, within the bound.
No kernel may reach another device: no remote copies, remote signals or barrier semaphores. Data moves between devices by JAX's collectives and lax.ppermute only.
A program may use at most 256 MiB of HBM per device.

v0:
```python
import jax
import jax.numpy as jnp
from jax import lax
from jax.sharding import PartitionSpec as P

HEAD_DIM = 64


def matmul(left, right):
    return jnp.dot(left, right, preferred_element_type=jnp.float32)


def matmul_tn(left, right):
    return lax.dot_general(
        left, right, (((0,), (0,)), ((), ())), preferred_element_type=jnp.float32
    )


def matmul_nt(left, right):
    return lax.dot_general(
        left, right, (((1,), (1,)), ((), ())), preferred_element_type=jnp.float32
    )


def layer_norm(summed, gain_vec, bias_vec):
    row_mean = jnp.mean(summed, axis=-1, keepdims=True)
    centred = summed - row_mean
    variance = jnp.mean(centred * centred, axis=-1, keepdims=True)
    inv_std = lax.rsqrt(variance + 1e-05)
    normed = centred * inv_std
    return (normed * gain_vec + bias_vec, normed, inv_std)


def norm_back(grad_out, normed, inv_std, gain_vec):
    grad_normed = grad_out * gain_vec
    centre_term = jnp.mean(grad_normed, axis=-1, keepdims=True)
    slope_term = jnp.mean(grad_normed * normed, axis=-1, keepdims=True)
    grad_in = inv_std * (grad_normed - centre_term - normed * slope_term)
    return (grad_in, jnp.sum(grad_out * normed, axis=0), jnp.sum(grad_out, axis=0))


def head_slice(matrix, head_index):
    return lax.dynamic_slice_in_dim(matrix, head_index * HEAD_DIM, HEAD_DIM, 1)


def head_merge(stacked):
    return jnp.transpose(stacked, (1, 0, 2)).reshape(
        stacked.shape[1], stacked.shape[0] * stacked.shape[2]
    )


def masked_scores(queries, key_rows, allowed):
    scores = matmul_nt(queries, key_rows) * HEAD_DIM ** (-0.5)
    return jnp.where(allowed, scores, -1e30)


def attend(queries, key_rows, value_rows, allowed):

    def per_head(head_index):
        scores = masked_scores(
            head_slice(queries, head_index), head_slice(key_rows, head_index), allowed
        )
        row_max = jnp.max(scores, axis=-1, keepdims=True)
        exp_scores = jnp.exp(scores - row_max)
        denominator = jnp.sum(exp_scores, axis=-1, keepdims=True)
        probs_low = (exp_scores / denominator).astype(jnp.bfloat16)
        mixture = matmul(probs_low, head_slice(value_rows, head_index))
        return (mixture, (row_max + jnp.log(denominator))[:, 0])

    mixture, log_sums = lax.map(per_head, jnp.arange(queries.shape[1] // HEAD_DIM))
    return (head_merge(mixture).astype(jnp.bfloat16), log_sums)


def attend_back(queries, key_rows, value_rows, allowed, log_sums, grad_mix):

    def per_head(head_index):
        head_q = head_slice(queries, head_index)
        head_k = head_slice(key_rows, head_index)
        head_v = head_slice(value_rows, head_index)
        head_g = head_slice(grad_mix, head_index)
        scores = masked_scores(head_q, head_k, allowed)
        probs = jnp.exp(scores - log_sums[head_index][:, None])
        grad_values = matmul_tn(probs.astype(jnp.bfloat16), head_g)
        grad_probs = matmul_nt(head_g, head_v)
        inner = jnp.sum(grad_probs * probs, axis=-1, keepdims=True)
        grad_scores = (probs * (grad_probs - inner) * HEAD_DIM ** (-0.5)).astype(jnp.bfloat16)
        return (matmul(grad_scores, head_k), matmul_tn(grad_scores, head_q), grad_values)

    grad_q, grad_k, grad_v = lax.map(per_head, jnp.arange(queries.shape[1] // HEAD_DIM))
    return (head_merge(grad_q), head_merge(grad_k), head_merge(grad_v))


def head_total(partial_value):
    return lax.psum(partial_value, "tensor")


def input_total(partial_value):
    return lax.psum(partial_value, "tensor")


def shards(
    x_in,
    lengths,
    retrieved,
    datastore,
    self_wq,
    self_wk,
    self_wv,
    self_wo,
    ln1_gain,
    ln1_bias,
    cross_wq,
    cross_wk,
    cross_wv,
    cross_wo,
    ln2_gain,
    ln2_bias,
    ffn_w1,
    ffn_w2,
    ln3_gain,
    ln3_bias,
    cotangent,
):
    bf_type = jnp.bfloat16
    token_count = x_in.shape[0]
    positions = lax.iota(jnp.int32, token_count)
    causal = positions[:, None] >= positions[None, :]
    x_float = x_in.astype(jnp.float32)
    q_self = matmul(x_in, self_wq).astype(bf_type)
    k_self = matmul(x_in, self_wk).astype(bf_type)
    v_self = matmul(x_in, self_wv).astype(bf_type)
    attn_self, lse_self = attend(q_self, k_self, v_self, causal)
    h_one, normed_one, inv_one = layer_norm(
        x_float + head_total(matmul(attn_self, self_wo)), ln1_gain, ln1_bias
    )
    h_one_low = h_one.astype(bf_type)
    q_cross = matmul(h_one_low, cross_wq).astype(bf_type)
    k_local = matmul(datastore, cross_wk).astype(bf_type)
    v_local = matmul(datastore, cross_wv).astype(bf_type)
    k_all, v_all = (
        lax.all_gather(k_local, "dp", axis=0, tiled=True),
        lax.all_gather(v_local, "dp", axis=0, tiled=True),
    )
    picked = (
        jnp.zeros((token_count, k_all.shape[0]), bool).at[positions[:, None], retrieved].set(True)
    )
    attn_cross, lse_cross = attend(q_cross, k_all, v_all, picked)
    h_two, normed_two, inv_two = layer_norm(
        h_one + head_total(matmul(attn_cross, cross_wo)), ln2_gain, ln2_bias
    )
    h_two_low = h_two.astype(bf_type)
    pre_act = matmul(h_two_low, ffn_w1)
    act_low = jax.nn.gelu(pre_act).astype(bf_type)
    h_three, normed_three, inv_three = layer_norm(
        h_two + head_total(matmul(act_low, ffn_w2)), ln3_gain, ln3_bias
    )
    row_valid = (positions < lengths[0]).astype(jnp.float32)[:, None]
    block_out = (h_three * row_valid).astype(bf_type)
    grad_out = cotangent.astype(jnp.float32) * row_valid
    d_three, grad_g3, grad_b3 = norm_back(grad_out, normed_three, inv_three, ln3_gain)
    e_three = d_three.astype(bf_type)
    grad_w2 = matmul_tn(act_low, e_three)
    d_act = matmul_nt(e_three, ffn_w2)
    unused, gelu_back = jax.vjp(jax.nn.gelu, pre_act)
    d_pre = gelu_back(d_act)[0].astype(bf_type)
    grad_w1 = matmul_tn(h_two_low, d_pre)
    d_h_two = d_three + input_total(matmul_nt(d_pre, ffn_w1))
    d_two, grad_g2, grad_b2 = norm_back(d_h_two, normed_two, inv_two, ln2_gain)
    e_two = d_two.astype(bf_type)
    grad_cwo = matmul_tn(attn_cross, e_two)
    d_mix_cross = matmul_nt(e_two, cross_wo).astype(bf_type)
    k_again = matmul(datastore, cross_wk).astype(bf_type)
    v_again = matmul(datastore, cross_wv).astype(bf_type)
    k_back, v_back = (
        lax.all_gather(k_again, "dp", axis=0, tiled=True),
        lax.all_gather(v_again, "dp", axis=0, tiled=True),
    )
    dq_cross, dk_cross, dv_cross = attend_back(
        q_cross, k_back, v_back, picked, lse_cross, d_mix_cross
    )
    dk_own, dv_own = (
        lax.psum_scatter(dk_cross, "dp", scatter_dimension=0, tiled=True),
        lax.psum_scatter(dv_cross, "dp", scatter_dimension=0, tiled=True),
    )
    dk_low = dk_own.astype(bf_type)
    dv_low = dv_own.astype(bf_type)
    grad_cwk = matmul_tn(datastore, dk_low)
    grad_cwv = matmul_tn(datastore, dv_low)
    store_part = matmul_nt(dk_low, cross_wk) + matmul_nt(dv_low, cross_wv)
    datastore_grad = lax.psum_scatter(
        store_part.astype(jnp.bfloat16), "tensor", scatter_dimension=1, tiled=True
    ).astype(jnp.float32)
    dq_cross_low = dq_cross.astype(bf_type)
    grad_cwq = matmul_tn(h_one_low, dq_cross_low)
    d_h_one = d_two + input_total(matmul_nt(dq_cross_low, cross_wq))
    d_one, grad_g1, grad_b1 = norm_back(d_h_one, normed_one, inv_one, ln1_gain)
    e_one = d_one.astype(bf_type)
    grad_swo = matmul_tn(attn_self, e_one)
    d_mix_self = matmul_nt(e_one, self_wo).astype(bf_type)
    dq_self, dk_self, dv_self = attend_back(q_self, k_self, v_self, causal, lse_self, d_mix_self)
    dq_low = dq_self.astype(bf_type)
    dk_low_self = dk_self.astype(bf_type)
    dv_low_self = dv_self.astype(bf_type)
    grad_swq = matmul_tn(x_in, dq_low)
    grad_swk = matmul_tn(x_in, dk_low_self)
    grad_swv = matmul_tn(x_in, dv_low_self)
    input_part = (
        matmul_nt(dq_low, self_wq)
        + matmul_nt(dk_low_self, self_wk)
        + matmul_nt(dv_low_self, self_wv)
    )
    input_grad = d_one + input_total(input_part)
    summed_grads = (
        lax.psum_scatter(grad_swq, "dp", scatter_dimension=0, tiled=True),
        lax.psum_scatter(grad_swk, "dp", scatter_dimension=0, tiled=True),
        lax.psum_scatter(grad_swv, "dp", scatter_dimension=0, tiled=True),
        lax.psum_scatter(grad_swo, "dp", scatter_dimension=1, tiled=True),
        lax.psum_scatter(grad_g1, "dp", scatter_dimension=0, tiled=True),
        lax.psum_scatter(grad_b1, "dp", scatter_dimension=0, tiled=True),
        lax.psum_scatter(grad_cwq, "dp", scatter_dimension=0, tiled=True),
        lax.psum_scatter(grad_cwk, "dp", scatter_dimension=0, tiled=True),
        lax.psum_scatter(grad_cwv, "dp", scatter_dimension=0, tiled=True),
        lax.psum_scatter(grad_cwo, "dp", scatter_dimension=1, tiled=True),
        lax.psum_scatter(grad_g2, "dp", scatter_dimension=0, tiled=True),
        lax.psum_scatter(grad_b2, "dp", scatter_dimension=0, tiled=True),
        lax.psum_scatter(grad_w1, "dp", scatter_dimension=0, tiled=True),
        lax.psum_scatter(grad_w2, "dp", scatter_dimension=1, tiled=True),
        lax.psum_scatter(grad_g3, "dp", scatter_dimension=0, tiled=True),
        lax.psum_scatter(grad_b3, "dp", scatter_dimension=0, tiled=True),
    )
    (
        s_swq,
        s_swk,
        s_swv,
        s_swo,
        s_g1,
        s_b1,
        s_cwq,
        s_cwk,
        s_cwv,
        s_cwo,
        s_g2,
        s_b2,
        s_w1,
        s_w2,
        s_g3,
        s_b3,
    ) = summed_grads
    return (
        block_out,
        input_grad,
        datastore_grad,
        s_swq,
        s_swk,
        s_swv,
        s_swo,
        s_g1,
        s_b1,
        s_cwq,
        s_cwk,
        s_cwv,
        s_cwo,
        s_g2,
        s_b2,
        s_w1,
        s_w2,
        s_g3,
        s_b3,
    )


def solution(mesh):
    in_specs = (
        P("dp", None),
        P("dp"),
        P("dp", None),
        P("dp", None),
        P(None, "tensor"),
        P(None, "tensor"),
        P(None, "tensor"),
        P("tensor", None),
        P(),
        P(),
        P(None, "tensor"),
        P(None, "tensor"),
        P(None, "tensor"),
        P("tensor", None),
        P(),
        P(),
        P(None, "tensor"),
        P("tensor", None),
        P(),
        P(),
        P("dp", None),
    )
    out_specs = (
        P("dp", None),
        P("dp", None),
        P("dp", "tensor"),
        P("dp", "tensor"),
        P("dp", "tensor"),
        P("dp", "tensor"),
        P("tensor", "dp"),
        P("dp"),
        P("dp"),
        P("dp", "tensor"),
        P("dp", "tensor"),
        P("dp", "tensor"),
        P("tensor", "dp"),
        P("dp"),
        P("dp"),
        P("dp", "tensor"),
        P("tensor", "dp"),
        P("dp"),
        P("dp"),
    )
    return jax.shard_map(shards, mesh=mesh, in_specs=in_specs, out_specs=out_specs, check_vma=False)
```

profile of v0, /device:TPU:0, one launch (start us, length us, event | category | flops | bytes accessed | tf_op | source)
XLA Modules:
  0.0 4500.5 jit_solution(9591030624200714795)
XLA Ops:
  13.2 20.3 while.56
  44.0 1090.8 %scatter_custom_fusion = pred[2097152]{0:T(1024)(128)(4,1)} fusion(s32[262144]{0:T(1024)} %bitcast.207, pred[262144]{0:T(1024)(128)(4,1)S(1)} %broadcast.164, pred[]{:T(512)} %constant.123.clone.1), kind=kCustom, calls=%fused_computation.89 | custom fusion | bytes 2097664
  1134.9 6.6 reshape.188
  1144.3 95.2 %while.54 = (s32[]{:T(128)}, bf16[6,256,64]{1,2,0:T(8,128)(2,1)S(1)}, f32[6,256]{1,0:T(8,128)S(1)}, s32[6]{0:T(128)S(1)}, bf16[256,384]{1,0:T(8,128)(2,1)S(1)}, ...) while((s32[]{:T(128)}, ...), condition=%wide.region_11.12_spmd, body=%wide.region_8.11_spmd.sunk | while | flops 553647872 | bytes 65154768 | solution.py:70
  1153.6 6.7 fusion.223
  1169.5 6.7 fusion.223
  1185.5 6.5 fusion.223
  1201.3 6.5 fusion.223
  1217.1 6.6 fusion.223
  1232.9 6.6 fusion.223
  1240.9 68.3 %all-reduce.31.cloned.1.call-done = f32[256,768]{1,0:T(8,128)} async-done(((f32[256,768]{1,0:T(8,128)}), f32[256,768]{1,0:T(8,128)}) %all-reduce.31.cloned.1.call-update) | async-done | bytes 786448 | tf_op jit(solution)/shard_map/psum | solution.py:94
  1316.0 62.8 %all-reduce.33.cloned.1.call-done = f32[256,768]{1,0:T(8,128)} async-done(((f32[256,768]{1,0:T(8,128)}), f32[256,768]{1,0:T(8,128)}) %all-reduce.33.cloned.1.call-update) | async-done | bytes 786448 | tf_op jit(solution)/shard_map/psum | solution.py:94
  1386.4 63.0 %all-reduce.35.cloned.1.call-done = f32[256,768]{1,0:T(8,128)} async-done(((f32[256,768]{1,0:T(8,128)}), f32[256,768]{1,0:T(8,128)}) %all-reduce.35.cloned.1.call-update) | async-done | bytes 786448 | tf_op jit(solution)/shard_map/psum | solution.py:98
  1455.2 200.4 %while.55 = (s32[]{:T(128)}, bf16[6,256,64]{1,2,0:T(8,128)(2,1)}, f32[6,8192,64]{1,2,0:T(8,128)}, f32[6,8192,64]{1,2,0:T(8,128)}, s32[6]{0:T(128)S(1)}, /*index=...) while((s32[]{:T(128)}, bf16[6,256,64]{1,2,0:T(8,128)(2,1)}, ...), condition=%wide.region_25.26_spmd, body=%wide.region_23.25_spmd.sunk | while | flops 1363148544 | bytes 144515952 | solution.py:89
  1462.6 8.0 multiply_reduce_fusion.16
  1470.6 7.8 multiply_convert_fusion.8
  1481.7 4.6 fusion.233
  1496.0 8.0 multiply_reduce_fusion.16
  1504.0 7.8 multiply_convert_fusion.8
  1515.1 4.6 fusion.233
  1529.4 8.0 multiply_reduce_fusion.16
  1537.4 7.8 multiply_convert_fusion.8
  1548.5 4.6 fusion.233
  1562.8 8.0 multiply_reduce_fusion.16
  1570.8 7.8 multiply_convert_fusion.8
  1581.8 4.6 fusion.233
  1596.2 8.0 multiply_reduce_fusion.16
  1604.2 7.8 multiply_convert_fusion.8
  1615.3 4.6 fusion.233
  1629.6 8.0 multiply_reduce_fusion.16
  1637.6 7.8 multiply_convert_fusion.8
  1648.7 4.6 fusion.233
  1658.2 12.7 copy.52
  1671.1 12.7 copy.50
  1688.0 35.1 all-reduce.37.cloned.1.call-done
  1725.7 37.3 while.57
  1771.9 637.0 %reduce-scatter.21.cloned.1.call-done = f32[64,384]{1,0:T(8,128)} async-done(((f32[8192,384]{1,0:T(8,128)}), f32[64,384]{1,0:T(8,128)}) %reduce-scatter.21.cloned.1.call-update) | async-done | bytes 98320
  2409.9 699.3 %reduce-scatter.19.cloned.1.call-done = f32[64,384]{1,0:T(8,128)} async-done(((f32[8192,384]{1,0:T(8,128)}), f32[64,384]{1,0:T(8,128)}) %reduce-scatter.19.cloned.1.call-update) | async-done | bytes 98320
  3123.6 397.1 %fusion.120 = (f32[8,1536]{1,0:T(8,128)S(1)}, f32[1536,8]{0,1:T(8,128)S(1)}) fusion(f32[768,1536]{1,0:T(8,128)} %fusion.111, f32[1536,768]{0,1:T(8,128)} %fusion.100), kind=kCustom, calls=%all-reduce-scatter.2 | all-reduce-scatter fusion | flops 3145729 | bytes 9536512
  3533.8 12.9 collective-permute-start.40
  3549.9 5.8 collective-permute-start.42
  3561.6 7.0 collective-permute-start.45
  3570.1 6.4 collective-permute-start.47
  3614.3 5.7 collective-permute-start.12
  3683.1 13.4 concatenate.5
  3696.6 48.9 %concatenate.4 = f32[262,1536]{1,0:T(8,128)} concatenate(f32[6,1536]{1,0:T(8,128)S(1)} %collective-permute-done.31, f32[8,1536]{1,0:T(8,128)} %copy-done.92, f32[8,1536]{1,0:T(8,128)} %copy-done.90, f32[8,1536]{1,0:T(8,128)} %copy-done.89, f32[8,1536]{1,0:T(8,128)} %copy-done.88, f32[8,1536]{1,0:T(8,128)} %copy-done.87, f32[8,1536]{1,0:T(8,128)} %copy-done.86, ...), dimensions={0} | concatenate | bytes 3219456
  3747.7 665.1 %all-reduce.18 = (f32[768]{0:T(1024)S(1)}, f32[768]{0:T(1024)S(1)}, f32[768]{0:T(1024)S(1)}, f32[768]{0:T(1024)S(1)}, f32[768]{0:T(1024)S(1)}, /*index=5*/f32[768]{0:T(1024)S(1)}) all-reduce(f32[768]{0:T(1024)S(1)} %get-tuple-element.311, f32[768]{0:T(1024)S(1)} %get-tuple-element.318, ...), channel_id=9, replica_groups=mesh['dp'=128,'tensor'=2] {'dp'}, use_global_device_ids=true, to_apply=%region_41.42.clone | all-reduce | flops 4608 | bytes 36864
  4420.2 59.4 %all-reduce.41.cloned.1.call-done = (f32[768,384]{0,1:T(8,128)}, f32[768,384]{0,1:T(8,128)}, f32[768,384]{0,1:T(8,128)}, f32[384,768]{0,1:T(8,128)}, f32[768,384...) async-done(((f32[768,384]{0,1:T(8,128)}, f32[768,384]{0,1:T(8,128)}, f32[768,384]{0,1:T(8,128)}, f32[384,768]{0,1:T(8,128)}, ...) | async-done | bytes 9437200
  (692 shorter events, 368.4 us)
Async XLA Ops:
  8.1 1133.4 %all-reduce.29.cloned.1.call-start = ((), (), s32[]{:S(2)}) async-start(), calls=%async_computation.3 | async-start | bytes 1572864 | tf_op jit(solution)/shard_map/psum | solution.py:94
  36.1 1108.1 %all-gather.3.cloned.1.call-start = ((), (), s32[]{:S(2)}) async-start(), calls=%async_computation.4 | async-start | bytes 6340608 | tf_op jit(solution)/shard_map/all_gather | solution.py:141
  38.1 1106.1 %all-gather.5.cloned.1.call-start = ((), (), s32[]{:S(2)}) async-start(), calls=%async_computation.5 | async-start | bytes 6340608 | tf_op jit(solution)/shard_map/all_gather | solution.py:142
  40.1 1269.0 %all-reduce.31.cloned.1.call-start = ((), (), s32[]{:S(2)}) async-start(), calls=%async_computation.6 | async-start | bytes 1572864 | tf_op jit(solution)/shard_map/psum | solution.py:94
  1240.8 137.9 %all-reduce.33.cloned.1.call-start = ((), (), s32[]{:S(2)}) async-start(), calls=%async_computation.7 | async-start | bytes 1572864 | tf_op jit(solution)/shard_map/psum | solution.py:94
  1315.2 134.1 %all-reduce.35.cloned.1.call-start = ((), (), s32[]{:S(2)}) async-start(), calls=%async_computation.8 | async-start | bytes 1572864 | tf_op jit(solution)/shard_map/psum | solution.py:98
  1385.9 337.2 %all-reduce.37.cloned.1.call-start = ((), (), s32[]{:S(2)}) async-start(), calls=%async_computation.9 | async-start | bytes 1572864 | tf_op jit(solution)/shard_map/psum | solution.py:98
  1658.1 750.7 %reduce-scatter.21.cloned.1.call-start = ((), (), s32[]{:S(2)}) async-start(), calls=%async_computation.12 | async-start | bytes 12681216
  1670.9 1438.3 %reduce-scatter.19.cloned.1.call-start = ((), (), s32[]{:S(2)}) async-start(), calls=%async_computation.11 | async-start | bytes 12681216
  1683.9 2732.4 %all-reduce.39.cloned.1.call-start = ((), (), s32[]{:S(2)}) async-start(), calls=%async_computation.10 | async-start | bytes 1572864 | tf_op jit(solution)/shard_map/psum | solution.py:98
  1770.5 2648.1 %reduce-scatter.23.cloned.1.call-start = ((), (), s32[]{:S(2)}) async-start(), calls=%async_computation.13 | async-start | bytes 294912
  3113.0 1366.6 %all-reduce.41.cloned.1.call-start = ((), (), s32[]{:S(2)}) async-start(), calls=%async_computation.14 | async-start | bytes 18874368
  3528.6 18.2 collective-permute-start.36
  3529.9 20.0 collective-permute-start.37
  3531.2 24.5 collective-permute-start.38
  3532.5 27.3 collective-permute-start.39
  3533.8 27.8 collective-permute-start.40
  3546.8 21.9 collective-permute-start.41
  3549.9 20.2 collective-permute-start.42
  3555.7 20.7 collective-permute-start.43
  3559.8 18.0 collective-permute-start.44
  3561.6 17.7 collective-permute-start.45
  3568.7 12.1 collective-permute-start.46
  3570.1 14.4 collective-permute-start.47
  3603.4 10.9 collective-permute-start.62
  3604.7 15.3 collective-permute-start
  3606.2 16.4 collective-permute-start.1
  3608.6 16.8 collective-permute-start.10
  3609.9 17.8 collective-permute-start.11
  3614.3 15.0 collective-permute-start.12
  3620.0 12.4 collective-permute-start.13
  3622.6 11.3 collective-permute-start.14
  3625.4 12.3 collective-permute-start.15
  3627.7 11.6 collective-permute-start.16
  3629.3 13.9 collective-permute-start.17
  3632.4 13.3 collective-permute-start.18
  3633.8 13.2 collective-permute-start.19
  3652.8 12.2 collective-permute-start.27
  3654.1 12.4 collective-permute-start.28
  3656.8 12.6 collective-permute-start.29
  3660.0 12.5 collective-permute-start.3
  3661.3 14.1 collective-permute-start.30
  3665.0 13.1 collective-permute-start.4
  3666.5 30.0 collective-permute-start.5
  3669.4 27.2 collective-permute-start.6
  3672.5 24.1 collective-permute-start.7
  3675.4 21.2 collective-permute-start.8
  3678.2 18.4 collective-permute-start.9
  (174 other events, 10228.3 us)
Sparse Core Ops, SparseCore 0:
  36.2 68.8 all-reduce.28
  1240.9 68.1 all-reduce.30
  1315.4 63.3 all-reduce.32
  1386.0 63.2 all-reduce.34
  1658.2 64.8 all-reduce.36
  1770.6 60.9 all-reduce.38
  3113.1 14.1 reduce-scatter.22
  3130.5 1349.0 all-reduce.40
Sparse Core Ops, SparseCore 1:
  39.2 230.6 all-gather.2
  272.4 205.0 all-gather.4
  1671.0 737.8 reduce-scatter.20
  2411.6 697.6 reduce-scatter.18
where the time goes:
time: 4520 us; the launch traced here: 4500 us
  waiting for transfers between devices  1630 us (36%)
  local copies, waits for them, and re-layouts  1250 us (28%)
  blocking collectives  1060 us (23%)
  matrix products  272 us (6%)
  starting transfers between devices  160 us (4%)
  other arithmetic  72.7 us (2%)
    unnamed x80, waiting for transfers between devices  1400 us
    unnamed x267, local copies, waits for them, and re-layouts  1210 us
    unnamed x2, blocking collectives  1060 us
    unnamed x68, starting transfers between devices  159 us
    psum x3, waiting for transfers between devices, head_total(): return lax.psum(partial_value, 'tensor')  131 us
    dot_general x46, matrix products, matmul_nt(): lax.dot_general(left, right, (((1,), (1,)), ((), ())), preferred_element_...  121 us
    psum x3, waiting for transfers between devices, input_total(): return lax.psum(partial_value, 'tensor')  98.1 us
    dot_general x34, matrix products, matmul(): return jnp.dot(left, right, preferred_element_type=jnp.float32)  94.4 us
  transfers between devices with their start and end apart: 76, of which 7 were waited for; matrix products, arithmetic and copies ran while one was open for 37% of the time, Pallas kernels for 0%

commit v1 on v0

v1 whole, which is shorter than its diff:
```python
import functools

import jax
import jax.numpy as jnp
from jax import lax
from jax.experimental import pallas as pl
from jax.experimental.pallas import tpu as pltpu
from jax.sharding import PartitionSpec as P

LOW = jnp.bfloat16
WIDE = jnp.float32
MASKED = -1e30
HEAD_DIM = 64
SCALE = 0.125
AXES = {"y": (4, 32), "x": (4, 8), "z": (4, 2), "core": (2, 1)}
N_DP = 128
VMEM = 48 * 2**20


def dot(left, right, left_dim=1, right_dim=0):
    return lax.dot_general(
        left, right, (((left_dim,), (right_dim,)), ((), ())), preferred_element_type=WIDE
    )


def coord(axis):
    size, stride = AXES[axis]
    return (lax.axis_index("dp") // stride) % size


def shift(value, axis, step):
    size, stride = AXES[axis]
    pairs = []
    for d in range(N_DP):
        at = (d // stride) % size
        pairs.append((d, d + ((at + step) % size - at) * stride))
    return lax.ppermute(value, "dp", pairs)


def other_tensor(value):
    return lax.ppermute(value, "tensor", [(0, 1), (1, 0)])


def tensor_total(partial_value):
    mine = partial_value.astype(LOW)
    return mine.astype(WIDE) + other_tensor(mine).astype(WIDE)


def gather(block, axis):
    return [block] + [shift(block, axis, k) for k in range(1, AXES[axis][0])]


def scatter_sum(pieces, axis):
    total = pieces[0].astype(WIDE)
    for k in range(1, len(pieces)):
        total = total + shift(pieces[k].astype(LOW), axis, -k).astype(WIDE)
    return total


def take_rows(value, index, size):
    return lax.dynamic_slice_in_dim(value, index * size, size, 0)


def weight_scatter(grads):
    n = grads.shape[1]
    half, quarter = n // 2, n // 4
    core = coord("core")
    grads = grads.astype(LOW)
    mine = lax.dynamic_slice_in_dim(grads, core * half, half, 1)
    theirs = lax.dynamic_slice_in_dim(grads, (1 - core) * half, half, 1)
    both = (mine.astype(WIDE) + shift(theirs, "core", 1).astype(WIDE)).astype(LOW)
    at_y, at_x, at_z = coord("y"), coord("x"), coord("z")
    one = both[:, :quarter]
    two = both[:, quarter:].reshape(4, 4, 48, quarter)
    one = scatter_sum([take_rows(one, (at_y - k) % 4, 192) for k in range(4)], "y")
    two = scatter_sum(
        [
            lax.dynamic_slice_in_dim(two, (at_x - k) % 4, 1, 1).reshape(192, quarter)
            for k in range(4)
        ],
        "x",
    )
    one = scatter_sum([take_rows(one, (at_x - k) % 4, 48) for k in range(4)], "x")
    two = scatter_sum([take_rows(two, (at_y - k) % 4, 48) for k in range(4)], "y")
    joined = jnp.concatenate([one, two], axis=1)
    joined = scatter_sum([take_rows(joined, (at_z - k) % 4, 12) for k in range(4)], "z")
    keep = take_rows(joined, core, 6)
    send = take_rows(joined, 1 - core, 6).astype(LOW)
    got = shift(send, "core", 1).astype(WIDE)
    first = jnp.where(core == 0, keep, got)
    second = jnp.where(core == 0, got, keep)
    return jnp.concatenate([first, second], axis=1)


def first_half_rows(pair, which):
    row = lax.broadcasted_iota(jnp.int32, pair.shape, 0)
    return jnp.where((row < HEAD_DIM) == (which == 0), pair, jnp.zeros_like(pair))


def first_half_lanes(pair, which):
    lane = lax.broadcasted_iota(jnp.int32, pair.shape, 1)
    return jnp.where((lane < HEAD_DIM) == (which == 0), pair, jnp.zeros_like(pair))


def mask_kernel(place_ref, picks_ref, out_ref, high_s, low_s, count_s):
    picks = picks_ref[...]
    core = (place_ref[3] - (picks >> 6)) & 1
    at_z = (place_ref[2] - (picks >> 7)) & 3
    at_x = (place_ref[1] - (picks >> 9)) & 3
    at_y = (place_ref[0] - (picks >> 11)) & 3
    high_s[...] = (core << 5) | (at_y << 3) | (at_x << 1) | (at_z >> 1)
    low_s[...] = ((at_z & 1) << 6) | (picks & 63)
    rows, k_top = picks_ref.shape

    def count(t, carry):
        high = high_s[pl.ds(t, 1), :]
        low = low_s[pl.ds(t, 1), :]
        is_high = lax.broadcasted_iota(jnp.int32, (64, k_top), 0) == high
        is_low = lax.broadcasted_iota(jnp.int32, (128, k_top), 0) == low
        count_s[pl.ds(pl.multiple_of(t * 64, 64), 64), :] = dot(
            jnp.where(is_high, 1.0, 0.0).astype(LOW), jnp.where(is_low, 1.0, 0.0).astype(LOW), 1, 1
        )
        return carry

    lax.fori_loop(0, rows, count, 0, unroll=4)

    def turn(h, carry):
        block = count_s[pl.ds(h, rows, stride=64), :]
        bias = jnp.where(block.T > 0.5, 0.0, MASKED)
        out_ref[pl.ds(pl.multiple_of(h * 128, 128), 128), :] = bias.astype(LOW)
        return carry

    lax.fori_loop(0, 64, turn, 0, unroll=2)


def cost(microseconds, moved):
    return pl.CostEstimate(
        flops=int(microseconds * 1e9), bytes_accessed=int(moved), transcendentals=0
    )


def retrieval_mask(place, picks):
    tokens, k_top = picks.shape
    rows = 128
    return pl.pallas_call(
        mask_kernel,
        out_shape=jax.ShapeDtypeStruct((8192, tokens), LOW),
        grid=(tokens // rows,),
        in_specs=[
            pl.BlockSpec(memory_space=pltpu.SMEM),
            pl.BlockSpec((rows, k_top), lambda i: (i, 0)),
        ],
        out_specs=pl.BlockSpec((8192, rows), lambda i: (0, i)),
        scratch_shapes=[
            pltpu.VMEM((rows, k_top), jnp.int32),
            pltpu.VMEM((rows, k_top), jnp.int32),
            pltpu.VMEM((rows * 64, 128), WIDE),
        ],
        compiler_params=pltpu.CompilerParams(vmem_limit_bytes=VMEM),
        cost_estimate=cost(43, 5e6),
        name="retrieval_mask",
    )(place, picks)


def cross_fwd_kernel(last, *refs):
    if last:
        qt_ref, k_ref, v_ref, bias_ref, acc_in, top_in, sum_in = refs[:7]
        mixt_ref, mix_ref, lse_ref, acc_s, top_s, sum_s = refs[7:]
    else:
        qt_ref, k_ref, v_ref, bias_ref = refs[:4]
        acc_s, top_s, sum_s = refs[4:]
    step = pl.program_id(0)

    @pl.when(step == 0)
    def start():
        if last:
            acc_s[...] = acc_in[...]
            top_s[...] = top_in[...]
            sum_s[...] = sum_in[...]
        else:
            acc_s[...] = jnp.zeros_like(acc_s)
            top_s[...] = jnp.full_like(top_s, MASKED)
            sum_s[...] = jnp.zeros_like(sum_s)

    bias = bias_ref[...].astype(WIDE)
    for pair in range(3):
        cols = slice(pair * 128, (pair + 1) * 128)
        keys, values, queries = k_ref[:, cols], v_ref[:, cols], qt_ref[cols, :]
        for a in range(2):
            h = 2 * pair + a
            rows = slice(h * HEAD_DIM, (h + 1) * HEAD_DIM)
            scores = dot(keys, first_half_rows(queries, a)) + bias
            old = top_s[h : h + 1, :]
            top = jnp.maximum(old, jnp.max(scores, axis=0, keepdims=True))
            fade = jnp.exp(old - top)
            weights = jnp.exp(scores - top)
            sum_s[h : h + 1, :] = sum_s[h : h + 1, :] * fade + jnp.sum(
                weights, axis=0, keepdims=True
            )
            top_s[h : h + 1, :] = top
            mixed = dot(values, weights.astype(LOW), 0, 0)
            acc_s[rows, :] = acc_s[rows, :] * fade + mixed[a * HEAD_DIM : (a + 1) * HEAD_DIM, :]

    if last:

        @pl.when(step == pl.num_programs(0) - 1)
        def finish():
            for h in range(6):
                rows = slice(h * HEAD_DIM, (h + 1) * HEAD_DIM)
                acc_s[rows, :] = acc_s[rows, :] / sum_s[h : h + 1, :]
            mixt_ref[...] = acc_s[...]
            mix_ref[...] = acc_s[...].T.astype(LOW)
            lse_ref[...] = top_s[...] + jnp.log(jnp.maximum(sum_s[...], 1e-30))


def cross_fwd(qt, keys, values, bias, offset, state=None, block=2048):
    states, tokens = keys.shape[0], qt.shape[1]
    last = state is not None
    whole = lambda i: (0, 0)
    rows = lambda i: (i, 0)
    skip = offset // block
    acc = jax.ShapeDtypeStruct((384, tokens), WIDE)
    row = jax.ShapeDtypeStruct((8, tokens), WIDE)
    state_specs = [pl.BlockSpec(a.shape, whole) for a in (acc, row, row)]
    in_specs = [
        pl.BlockSpec((384, tokens), whole),
        pl.BlockSpec((block, 384), rows),
        pl.BlockSpec((block, 384), rows),
        pl.BlockSpec((block, tokens), lambda i: (i + skip, 0)),
    ]
    scratch = []
    args = (qt, keys, values, bias)
    if last:
        in_specs += state_specs
        args += state
        out_shape = (acc, jax.ShapeDtypeStruct((tokens, 384), LOW), row)
        out_specs = [pl.BlockSpec(a.shape, whole) for a in out_shape]
        scratch = [pltpu.VMEM(a.shape, WIDE) for a in (acc, row, row)]
    else:
        out_shape, out_specs = (acc, row, row), state_specs
    return pl.pallas_call(
        functools.partial(cross_fwd_kernel, last),
        out_shape=out_shape,
        grid=(states // block,),
        in_specs=in_specs,
        out_specs=out_specs,
        scratch_shapes=scratch,
        compiler_params=pltpu.CompilerParams(vmem_limit_bytes=VMEM),
        cost_estimate=cost(15, 8e6),
        name="cross_fwd",
    )(*args)


def cross_bwd_kernel(
    qt_ref,
    q_ref,
    dmt_ref,
    dm_ref,
    lse_ref,
    inner_ref,
    dq_in,
    k_ref,
    v_ref,
    bias_ref,
    dk_ref,
    dv_ref,
    dq_ref,
):
    @pl.when(pl.program_id(0) == 0)
    def start():
        dq_ref[...] = dq_in[...]

    bias = bias_ref[...].astype(WIDE)
    for pair in range(3):
        cols = slice(pair * 128, (pair + 1) * 128)
        keys, values = k_ref[:, cols], v_ref[:, cols]
        dk = dv = None
        for a in range(2):
            h = 2 * pair + a
            rows = slice(h * HEAD_DIM, (h + 1) * HEAD_DIM)
            scores = dot(keys, first_half_rows(qt_ref[cols, :], a)) + bias
            probs = jnp.exp(scores - lse_ref[h : h + 1, :])
            dp = dot(values, first_half_rows(dmt_ref[cols, :], a))
            ds = (probs * (dp - inner_ref[h : h + 1, :])).astype(LOW)
            dv_head = dot(probs.astype(LOW), first_half_lanes(dm_ref[:, cols], a))
            dk_head = dot(ds, first_half_lanes(q_ref[:, cols], a))
            dk = dk_head if a == 0 else dk + dk_head
            dv = dv_head if a == 0 else dv + dv_head
            dq = dot(keys, ds, 0, 0)
            dq_ref[rows, :] += dq[a * HEAD_DIM : (a + 1) * HEAD_DIM, :]
        dk_ref[:, cols] = dk.astype(LOW)
        dv_ref[:, cols] = dv.astype(LOW)


def cross_bwd(qt, q, dmt, dm, lse, inner, dq, keys, values, bias, offset, block=1024):
    states, tokens = keys.shape[0], qt.shape[1]
    whole = lambda i: (0, 0)
    rows = lambda i: (i, 0)
    skip = offset // block
    return pl.pallas_call(
        cross_bwd_kernel,
        out_shape=(
            jax.ShapeDtypeStruct((states, 384), LOW),
            jax.ShapeDtypeStruct((states, 384), LOW),
            jax.ShapeDtypeStruct((384, tokens), WIDE),
        ),
        grid=(states // block,),
        in_specs=[
            pl.BlockSpec((384, tokens), whole),
            pl.BlockSpec((tokens, 384), whole),
            pl.BlockSpec((384, tokens), whole),
            pl.BlockSpec((tokens, 384), whole),
            pl.BlockSpec((8, tokens), whole),
            pl.BlockSpec((8, tokens), whole),
            pl.BlockSpec((384, tokens), whole),
            pl.BlockSpec((block, 384), rows),
            pl.BlockSpec((block, 384), rows),
            pl.BlockSpec((block, tokens), lambda i: (i + skip, 0)),
        ],
        out_specs=(
            pl.BlockSpec((block, 384), rows),
            pl.BlockSpec((block, 384), rows),
            pl.BlockSpec((384, tokens), whole),
        ),
        compiler_params=pltpu.CompilerParams(vmem_limit_bytes=VMEM),
        cost_estimate=cost(18, 14e6),
        name="cross_bwd",
    )(qt, q, dmt, dm, lse, inner, dq, keys, values, bias)


def causal_bias(tokens):
    key = lax.broadcasted_iota(jnp.int32, (tokens, tokens), 0)
    query = lax.broadcasted_iota(jnp.int32, (tokens, tokens), 1)
    return jnp.where(key <= query, 0.0, MASKED)


def self_fwd_kernel(
    x_ref, wq_ref, wk_ref, wv_ref, wo_ref, q_ref, k_ref, v_ref, mixt_ref, mix_ref, lse_ref, part_ref
):
    x = x_ref[...]
    tokens = x.shape[0]
    q_ref[...] = dot(x, wq_ref[...]).astype(LOW) * jnp.asarray(SCALE, LOW)
    k_ref[...] = dot(x, wk_ref[...]).astype(LOW)
    v_ref[...] = dot(x, wv_ref[...]).astype(LOW)
    bias = causal_bias(tokens)
    lse_ref[...] = jnp.zeros_like(lse_ref)
    for pair in range(3):
        cols = slice(pair * 128, (pair + 1) * 128)
        queries, keys, values = q_ref[:, cols], k_ref[:, cols], v_ref[:, cols]
        for a in range(2):
            h = 2 * pair + a
            scores = dot(keys, first_half_lanes(queries, a), 1, 1) + bias
            top = jnp.max(scores, axis=0, keepdims=True)
            weights = jnp.exp(scores - top)
            total = jnp.sum(weights, axis=0, keepdims=True)
            mixed = dot(values, weights.astype(LOW), 0, 0)[a * HEAD_DIM : (a + 1) * HEAD_DIM, :]
            mixt_ref[h * HEAD_DIM : (h + 1) * HEAD_DIM, :] = mixed / total
            lse_ref[h : h + 1, :] = top + jnp.log(total)
    mix_ref[...] = mixt_ref[...].T.astype(LOW)
    part_ref[...] = dot(mix_ref[...], wo_ref[...]).astype(LOW)


def self_fwd(x, wq, wk, wv, wo):
    tokens = x.shape[0]
    narrow = jax.ShapeDtypeStruct((tokens, 384), LOW)
    return pl.pallas_call(
        self_fwd_kernel,
        out_shape=(
            narrow,
            narrow,
            narrow,
            jax.ShapeDtypeStruct((384, tokens), WIDE),
            narrow,
            jax.ShapeDtypeStruct((8, tokens), WIDE),
            jax.ShapeDtypeStruct((tokens, 768), LOW),
        ),
        compiler_params=pltpu.CompilerParams(vmem_limit_bytes=VMEM),
        cost_estimate=cost(8, 4e6),
        name="self_fwd",
    )(x, wq, wk, wv, wo)


def self_bwd_kernel(
    e_ref,
    q_ref,
    k_ref,
    v_ref,
    mixt_ref,
    lse_ref,
    wq_ref,
    wk_ref,
    wv_ref,
    wo_ref,
    dq_ref,
    dk_ref,
    dv_ref,
    part_ref,
    dqt_s,
):
    tokens = e_ref.shape[0]
    dm = dot(e_ref[...], wo_ref[...], 1, 1).astype(LOW)
    dmt = dm.astype(WIDE).T
    bias = causal_bias(tokens)
    for pair in range(3):
        cols = slice(pair * 128, (pair + 1) * 128)
        queries, keys, values, dm_pair = q_ref[:, cols], k_ref[:, cols], v_ref[:, cols], dm[:, cols]
        dk = dv = None
        for a in range(2):
            h = 2 * pair + a
            rows = slice(h * HEAD_DIM, (h + 1) * HEAD_DIM)
            q_head = first_half_lanes(queries, a)
            dm_head = first_half_lanes(dm_pair, a)
            inner = jnp.sum(dmt[rows, :] * mixt_ref[rows, :], axis=0, keepdims=True)
            scores = dot(keys, q_head, 1, 1) + bias
            probs = jnp.exp(scores - lse_ref[h : h + 1, :])
            dp = dot(values, dm_head, 1, 1)
            ds = (probs * (dp - inner)).astype(LOW)
            dv_head = dot(probs.astype(LOW), dm_head)
            dk_head = dot(ds, q_head)
            dk = dk_head if a == 0 else dk + dk_head
            dv = dv_head if a == 0 else dv + dv_head
            dqt_s[rows, :] = dot(keys, ds, 0, 0)[a * HEAD_DIM : (a + 1) * HEAD_DIM, :] * SCALE
        dk_ref[:, cols] = dk.astype(LOW)
        dv_ref[:, cols] = dv.astype(LOW)
    dq_ref[...] = dqt_s[...].T.astype(LOW)
    part_ref[...] = (
        dot(dq_ref[...], wq_ref[...], 1, 1)
        + dot(dk_ref[...], wk_ref[...], 1, 1)
        + dot(dv_ref[...], wv_ref[...], 1, 1)
    ).astype(LOW)


def self_bwd(e_one, q, k, v, mixt, lse, wq, wk, wv, wo):
    tokens = e_one.shape[0]
    narrow = jax.ShapeDtypeStruct((tokens, 384), LOW)
    return pl.pallas_call(
        self_bwd_kernel,
        out_shape=(narrow, narrow, narrow, jax.ShapeDtypeStruct((tokens, 768), LOW)),
        scratch_shapes=[pltpu.VMEM((384, tokens), WIDE)],
        compiler_params=pltpu.CompilerParams(vmem_limit_bytes=VMEM),
        cost_estimate=cost(10, 5e6),
        name="self_bwd",
    )(e_one, q, k, v, mixt, lse, wq, wk, wv, wo)


def layer_norm(summed, gain_vec, bias_vec):
    row_mean = jnp.mean(summed, axis=-1, keepdims=True)
    centred = summed - row_mean
    variance = jnp.mean(centred * centred, axis=-1, keepdims=True)
    inv_std = lax.rsqrt(variance + 1e-05)
    normed = centred * inv_std
    return (normed * gain_vec + bias_vec, normed, inv_std)


def norm_back(grad_out, normed, inv_std, gain_vec):
    grad_normed = grad_out * gain_vec
    centre_term = jnp.mean(grad_normed, axis=-1, keepdims=True)
    slope_term = jnp.mean(grad_normed * normed, axis=-1, keepdims=True)
    grad_in = inv_std * (grad_normed - centre_term - normed * slope_term)
    return (grad_in, jnp.sum(grad_out * normed, axis=0), jnp.sum(grad_out, axis=0))


def shards(
    x_in,
    lengths,
    retrieved,
    datastore,
    self_wq,
    self_wk,
    self_wv,
    self_wo,
    ln1_gain,
    ln1_bias,
    cross_wq,
    cross_wk,
    cross_wv,
    cross_wo,
    ln2_gain,
    ln2_bias,
    ffn_w1,
    ffn_w2,
    ln3_gain,
    ln3_bias,
    cotangent,
):
    tokens = x_in.shape[0]
    positions = lax.iota(jnp.int32, tokens)

    k_own = dot(datastore, cross_wk).astype(LOW)
    v_own = dot(datastore, cross_wv).astype(LOW)
    for axis in ("z", "x", "y"):
        k_own = jnp.concatenate(gather(k_own, axis), axis=0)
    v_own = jnp.concatenate(gather(v_own, "z"), axis=0)
    v_own = jnp.concatenate(gather(v_own, "y"), axis=0).reshape(4, 1, 256, 384)
    v_own = jnp.concatenate(gather(v_own, "x"), axis=1).reshape(4096, 384)
    k_far, v_far = shift(k_own, "core", 1), shift(v_own, "core", 1)

    q_self, k_self, v_self, mixt_self, mix_self, lse_self, part = self_fwd(
        x_in, self_wq, self_wk, self_wv, self_wo
    )
    place = jnp.stack([coord("y"), coord("x"), coord("z"), coord("core")]).astype(jnp.int32)
    bias = retrieval_mask(place, retrieved)
    h_one, normed_one, inv_one = layer_norm(
        x_in.astype(WIDE) + tensor_total(part), ln1_gain, ln1_bias
    )
    h_one_low = h_one.astype(LOW)
    q_cross = dot(h_one_low, cross_wq).astype(LOW) * jnp.asarray(SCALE, LOW)
    qt_cross = q_cross.T
    state = cross_fwd(qt_cross, k_own, v_own, bias, 0)
    mixt_cross, mix_cross, lse_cross = cross_fwd(qt_cross, k_far, v_far, bias, 4096, tuple(state))
    h_two, normed_two, inv_two = layer_norm(
        h_one + tensor_total(dot(mix_cross, cross_wo)), ln2_gain, ln2_bias
    )
    h_two_low = h_two.astype(LOW)
    pre_act = dot(h_two_low, ffn_w1)
    act_low = jax.nn.gelu(pre_act).astype(LOW)
    h_three, normed_three, inv_three = layer_norm(
        h_two + tensor_total(dot(act_low, ffn_w2)), ln3_gain, ln3_bias
    )
    row_valid = (positions < lengths[0]).astype(WIDE)[:, None]
    block_out = (h_three * row_valid).astype(LOW)

    grad_out = cotangent.astype(WIDE) * row_valid
    d_three, grad_g3, grad_b3 = norm_back(grad_out, normed_three, inv_three, ln3_gain)
    e_three = d_three.astype(LOW)
    d_act = dot(e_three, ffn_w2, 1, 1)
    unused, gelu_back = jax.vjp(jax.nn.gelu, pre_act)
    d_pre = gelu_back(d_act)[0].astype(LOW)
    d_h_two = d_three + tensor_total(dot(d_pre, ffn_w1, 1, 1))
    grads_ffn = jnp.concatenate(
        [dot(h_two_low, d_pre, 0, 0).astype(LOW), dot(e_three, act_low, 0, 0).astype(LOW)], axis=1
    )
    d_two, grad_g2, grad_b2 = norm_back(d_h_two, normed_two, inv_two, ln2_gain)
    e_two = d_two.astype(LOW)
    dm_cross = dot(e_two, cross_wo, 1, 1).astype(LOW)
    dmt_cross = dm_cross.T
    inner = jnp.sum((dmt_cross.astype(WIDE) * mixt_cross).reshape(6, HEAD_DIM, tokens), axis=1)
    inner = jnp.concatenate([inner, jnp.zeros((2, tokens), WIDE)], axis=0)
    sides = (qt_cross, q_cross, dmt_cross, dm_cross, lse_cross, inner)
    dk_far, dv_far, dqt = cross_bwd(
        *sides, jnp.zeros((384, tokens), WIDE), k_far, v_far, bias, 4096
    )
    dk_got, dv_got = shift(dk_far, "core", 1), shift(dv_far, "core", 1)
    dk_own, dv_own, dqt = cross_bwd(*sides, dqt, k_own, v_own, bias, 0)
    dqt_low = (dqt * SCALE).astype(LOW)
    d_h_one = d_two + tensor_total(dot(dqt_low, cross_wq, 0, 1))

    ffn_sum = weight_scatter(grads_ffn)

    dk = (dk_own.astype(WIDE) + dk_got.astype(WIDE)).astype(LOW)
    dv = (dv_own.astype(WIDE) + dv_got.astype(WIDE)).astype(LOW)
    dk = scatter_sum([dk[k * 1024 : (k + 1) * 1024] for k in range(4)], "y")
    dv = dv.reshape(4, 4, 256, 384)
    dv = scatter_sum([dv[:, k].reshape(1024, 384) for k in range(4)], "x")
    dk = scatter_sum([dk[k * 256 : (k + 1) * 256] for k in range(4)], "x")
    dv = scatter_sum([dv[k * 256 : (k + 1) * 256] for k in range(4)], "y")
    dk_low = scatter_sum([dk[k * 64 : (k + 1) * 64] for k in range(4)], "z").astype(LOW)
    dv_low = scatter_sum([dv[k * 64 : (k + 1) * 64] for k in range(4)], "z").astype(LOW)
    store_part = dot(dk_low, cross_wk, 1, 1) + dot(dv_low, cross_wv, 1, 1)
    tensor_at = lax.axis_index("tensor")
    store_mine = lax.dynamic_slice_in_dim(store_part, tensor_at * 384, 384, 1)
    store_send = lax.dynamic_slice_in_dim(store_part, (1 - tensor_at) * 384, 384, 1)
    datastore_grad = store_mine + other_tensor(store_send.astype(LOW)).astype(WIDE)
    store_sum = weight_scatter(
        jnp.concatenate([dot(datastore, dk_low, 0, 0), dot(datastore, dv_low, 0, 0)], axis=1)
    )

    d_one, grad_g1, grad_b1 = norm_back(d_h_one, normed_one, inv_one, ln1_gain)
    e_one = d_one.astype(LOW)
    dq_self, dk_self, dv_self, part = self_bwd(
        e_one,
        q_self,
        k_self,
        v_self,
        mixt_self,
        lse_self,
        self_wq,
        self_wk,
        self_wv,
        self_wo,
    )
    input_grad = d_one + tensor_total(part)
    vectors = jnp.stack([grad_g1, grad_b1, grad_g2, grad_b2, grad_g3, grad_b3], axis=1)
    grads = [
        dot(x_in, dq_self, 0, 0),
        dot(x_in, dk_self, 0, 0),
        dot(x_in, dv_self, 0, 0),
        dot(e_one, mix_self, 0, 0),
        dot(h_one_low, dqt_low, 0, 1),
        dot(e_two, mix_cross, 0, 0),
        jnp.pad(vectors, ((0, 0), (0, 250))),
    ]
    late_sum = weight_scatter(jnp.concatenate([g.astype(LOW) for g in grads], axis=1))
    part_of = lambda k: late_sum[:, k * 384 : (k + 1) * 384]
    vector = lambda k: late_sum[:, 2304 + k]
    return (
        block_out,
        input_grad,
        datastore_grad,
        part_of(0),
        part_of(1),
        part_of(2),
        part_of(3).T,
        vector(0),
        vector(1),
        part_of(4),
        store_sum[:, :384],
        store_sum[:, 384:],
        part_of(5).T,
        vector(2),
        vector(3),
        ffn_sum[:, :1536],
        ffn_sum[:, 1536:].T,
        vector(4),
        vector(5),
    )


def solution(mesh):
    rows, columns, split = P("dp", None), P(None, "tensor"), P("tensor", None)
    norm = (P(), P())
    in_specs = (
        (rows, P("dp"), rows, rows)
        + (columns, columns, columns, split)
        + norm
        + (columns, columns, columns, split)
        + norm
        + (columns, split)
        + norm
        + (rows,)
    )
    both, turned, vector = P("dp", "tensor"), P("tensor", "dp"), P("dp")
    out_specs = (
        (rows, rows, both)
        + (both, both, both, turned)
        + (vector, vector)
        + (both, both, both, turned)
        + (vector, vector)
        + (both, turned)
        + (vector, vector)
    )
    return jax.shard_map(shards, mesh=mesh, in_specs=in_specs, out_specs=out_specs, check_vma=False)
```

time: 4520 us -> 561 us (0.12)
  waiting for transfers between devices: 1630 us -> 176 us
  local copies, waits for them, and re-layouts: 1250 us -> 30.1 us
  blocking collectives: 1060 us -> 0 us
  matrix products: 272 us -> 19.8 us
  Pallas kernels: 0 us -> 117 us
    unnamed x80 -> x0, waiting for transfers between devices: 1400 us -> none
    unnamed x267 -> x202, local copies, waits for them, and re-layouts: 1210 us -> 17.4 us
    unnamed x2 -> x0, blocking collectives: 1060 us -> none
    dot_general x114 -> x22, matrix products: 272 us -> 19.8 us  [dot(): lax.dot_general(left, right, (((left_dim,), (right_dim,)), ((), ())), pre...]
    psum x6 -> x0, waiting for transfers between devices: 229 us -> none  [the longest x3 131 us: head_total(): return lax.psum(partial_value, 'tensor')]
    ppermute x0 -> x98, waiting for transfers between devices: none -> 176 us  [the longest x91 125 us: shift(): return lax.ppermute(value, 'dp', pairs)]
    ppermute x0 -> x98, starting transfers between devices: none -> 170 us  [the longest x91 130 us: shift(): return lax.ppermute(value, 'dp', pairs)]
    unnamed x68 -> x0, starting transfers between devices: 159 us -> none
  transfers between devices with their start and end apart: 76 -> 98, of which waited for: 7 -> 44; matrix products, arithmetic and copies ran while one was open for 37% -> 11% of each run, Pallas kernels for 0% -> 12%
where the time goes in v1:
time: 561 us; the launch traced here: 551 us
  waiting for transfers between devices  176 us (31%)
  starting transfers between devices  170 us (30%)
  Pallas kernels  117 us (21%)
  other arithmetic  34.6 us (6%)
  local copies, waits for them, and re-layouts  30.1 us (5%)
  matrix products  19.8 us (4%)
    ppermute x91, starting transfers between devices, shift(): return lax.ppermute(value, 'dp', pairs)  130 us
    ppermute x91, waiting for transfers between devices, shift(): return lax.ppermute(value, 'dp', pairs)  125 us
    ppermute x7, waiting for transfers between devices, other_tensor(): return lax.ppermute(value, 'tensor', [(0, 1), (1, 0)])  50.3 us
    pallas_call x1, Pallas kernels, retrieval_mask(): pl.pallas_call(mask_kernel, out_shape=jax.ShapeDtypeStruct((8192, tokens)...  42.6 us
    ppermute x7, starting transfers between devices, other_tensor(): return lax.ppermute(value, 'tensor', [(0, 1), (1, 0)])  40 us
    pallas_call x2, Pallas kernels, cross_bwd(): pl.pallas_call(cross_bwd_kernel, out_shape=(jax.ShapeDtypeStruct((states,...  36.5 us
    pallas_call x2, Pallas kernels, cross_fwd(): pl.pallas_call(functools.partial(cross_fwd_kernel, last), out_shape=out_s...  31.9 us
    dot_general x22, matrix products, dot(): lax.dot_general(left, right, (((left_dim,), (right_dim,)), ((), ())), pre...  19.8 us
  transfers between devices with their start and end apart: 98, of which 44 were waited for; matrix products, arithmetic and copies ran while one was open for 11% of the time, Pallas kernels for 12%

profile of v1, /device:TPU:0, one launch (start us, length us, event | category | flops | bytes accessed | tf_op | source)
XLA Modules:
  0.0 550.7 jit_solution(3256895728458555105)
XLA Ops:
  3.0 3.3 collective-permute-start.2
  19.4 3.3 collective-permute-done.4
  38.3 16.1 %collective-permute-done.14 = bf16[256,384]{1,0:T(8,128)(2,1)S(1)} collective-permute-done((bf16[256,384]{1,0:T(8,128)(2,1)S(1)}, bf16[256,384]{1,0:T(8,128)(2,1)S(1)}, u32[]{:S(2)}, u32[]{:S(2)}) %collective-permute-start.14) | collective-permute-done | bytes 196640 | tf_op jit(solution)/shard_map/ppermute | solution.py:37
  57.3 2.9 collective-permute-done.15
  61.9 3.8 collective-permute-start.18
  74.3 5.7 %collective-permute-start = (bf16[256,768]{1,0:T(8,128)(2,1)S(1)}, bf16[256,768]{1,0:T(8,128)(2,1)S(1)}, u32[]{:S(2)}, u32[]{:S(2)}) collective-permute-start(bf16[256,768]{1,0:T(8,128)(2,1)S(1)} %get-tuple-element.42), channel_id=1, source_target_pairs={{0,1},{1,0},{2,3},{3,2},{4,5},{5,4},{6,7},{7,6},{8,9},{9,8},{10,11... | collective-permute-start | bytes 1179656 | tf_op jit(solution)/shard_map/ppermute | solution.py:41
  84.2 4.9 collective-permute-done.18
  89.1 3.3 pad_maximum_fusion
  92.8 42.6 %retrieval_mask.1.refs_3_.bias_ref = bf16[8192,256]{1,0:T(8,128)(2,1)S(1)} custom-call(s32[4]{0:T(128)S(1)} %pad_add_fusion.place_ref, s32[256,1024]{1,0:T(8,128)S(1)} %copy-done.10), custom_call_target="tpu_custom_call" | custom-call | flops 43000000512 | bytes 5000000 | tf_op jit(solution)/shard_map/retrieval_mask/pallas_call | solution.py:145
  137.8 15.8 %cross_fwd.2 = (f32[384,256]{1,0:T(8,128)S(1)}, f32[8,256]{1,0:T(8,128)S(1)}, f32[8,256]{1,0:T(8,128)S(1)}) custom-call(bf16[384,256]{1,0:T(8,128)(2,1)S(1)} %copy.110.refs_0_.qt_ref, bf16[4096,384]{1,0:T(8,128)(2,1)} %constant_dynamic-update-slice_fusion.7.refs_1_.k_ref, bf16[4096,384]{1,0:T(8,128)(2,1)} %bitcast.6.refs_2_.v_ref, bf16[8192,256]{1,0:T(8,128)(2,1)} %copy-done.19), custom_call_target="tpu_custom_call" | custom-call | flops 15000000512 | bytes 8000000 | tf_op jit(solution)/shard_map/cross_fwd/pallas_call | solution.py:241
  154.7 16.2 %cross_fwd.3 = (f32[384,256]{1,0:T(8,128)S(1)}, bf16[256,384]{1,0:T(8,128)(2,1)S(1)}, f32[8,256]{1,0:T(8,128)S(1)}) custom-call(bf16[384,256]{1,0:T(8,128)(2,1)S(1)} %copy-done.8, bf16[4096,384]{1,0:T(8,128)(2,1)} %collective-permute-done.10.refs_1_.k_ref, bf16[4096,384]{1,0:T(8,128)(2,1)} %collective-permute-done.20.refs_2_.v_ref, ...), custom_call_target="tpu_custom_call" | custom-call | flops 15000000512 | bytes 8000000 | tf_op jit(solution)/shard_map/cross_fwd/pallas_call | solution.py:241
  171.2 5.8 %collective-permute-start.21 = (bf16[256,768]{1,0:T(8,128)(2,1)S(1)}, bf16[256,768]{1,0:T(8,128)(2,1)S(1)}, u32[]{:S(2)}, u32[]{:S(2)}) collective-permute-start(bf16[256,768]{1,0:T(8,128)(2,1)S(1)} %convolution_convert_fusion.13), channel_id=1, source_target_pairs={{0,1},{1,0},{2,3},{3,2},{4,5},{5,4},{6,7},{7,6},{8,9},{9,8},{10,11... | collective-permute-start | bytes 1179656 | tf_op jit(solution)/shard_map/ppermute | solution.py:41
  177.1 10.9 %collective-permute-done.21 = bf16[256,768]{1,0:T(8,128)(2,1)S(1)} collective-permute-done((bf16[256,768]{1,0:T(8,128)(2,1)S(1)}, bf16[256,768]{1,0:T(8,128)(2,1)S(1)}, u32[]{:S(2)}, u32[]{:S(2)}) %collective-permute-start.21) | collective-permute-done | bytes 393248 | tf_op jit(solution)/shard_map/ppermute | solution.py:41
  190.6 12.4 %collective-permute-start.22 = (bf16[256,768]{1,0:T(8,128)(2,1)S(1)}, bf16[256,768]{1,0:T(8,128)(2,1)S(1)}, u32[]{:S(2)}, u32[]{:S(2)}) collective-permute-start(bf16[256,768]{1,0:T(8,128)(2,1)S(1)} %convolution_convert_fusion.11), channel_id=1, source_target_pairs={{0,1},{1,0},{2,3},{3,2},{4,5},{5,4},{6,7},{7,6},{8,9},{9,8},{10,11... | collective-permute-start | bytes 1179656 | tf_op jit(solution)/shard_map/ppermute | solution.py:41
  203.7 12.2 %collective-permute-done.22 = bf16[256,768]{1,0:T(8,128)(2,1)S(1)} collective-permute-done((bf16[256,768]{1,0:T(8,128)(2,1)S(1)}, bf16[256,768]{1,0:T(8,128)(2,1)S(1)}, u32[]{:S(2)}, u32[]{:S(2)}) %collective-permute-start.22) | collective-permute-done | bytes 393248 | tf_op jit(solution)/shard_map/ppermute | solution.py:41
  220.8 7.0 %collective-permute-start.23 = (bf16[256,768]{1,0:T(8,128)(2,1)}, bf16[256,768]{1,0:T(8,128)(2,1)}, u32[]{:S(2)}, u32[]{:S(2)}) collective-permute-start(bf16[256,768]{1,0:T(8,128)(2,1)} %convolution_convert_fusion.10), channel_id=1, source_target_pairs={{0,1},{1,0},{2,3},{3,2},{4,5},{5,4},{6,7},{7,6},{8,9},{9,8},{10,11... | collective-permute-start | bytes 1179656 | tf_op jit(solution)/shard_map/ppermute | solution.py:41
  228.9 4.5 convolution_convert_fusion
  233.4 8.3 %collective-permute-done.23 = bf16[256,768]{1,0:T(8,128)(2,1)} collective-permute-done((bf16[256,768]{1,0:T(8,128)(2,1)}, bf16[256,768]{1,0:T(8,128)(2,1)}, u32[]{:S(2)}, u32[]{:S(2)}) %collective-permute-start.23) | collective-permute-done | bytes 393248 | tf_op jit(solution)/shard_map/ppermute | solution.py:41
  248.3 18.3 %cross_bwd.2 = (bf16[4096,384]{1,0:T(8,128)(2,1)}, bf16[4096,384]{1,0:T(8,128)(2,1)}, f32[384,256]{1,0:T(8,128)S(1)}) custom-call(bf16[384,256]{1,0:T(8,128)(2,1)S(1)} %copy-done.9, bf16[256,384]{1,0:T(8,128)(2,1)S(1)} %copy-done.6, bf16[384,256]{1,0:T(8,128)(2,1)S(1)} %copy.116.dmt_ref, bf16[256,384]{1,0:T(8,128)(2,1)S(1)} %convolution_convert_fusion.14.dm_ref, ...), custom_call_target="tpu_custom_call" | custom-call | flops 17999998976 | bytes 14000000 | tf_op jit(solution)/shard_map/cross_bwd/pallas_call | solution.py:300
  266.6 18.1 %cross_bwd.3 = (bf16[4096,384]{1,0:T(8,128)(2,1)S(1)}, bf16[4096,384]{1,0:T(8,128)(2,1)}, f32[384,256]{1,0:T(8,128)S(1)}) custom-call(bf16[384,256]{1,0:T(8,128)(2,1)S(1)} %copy-done.9, bf16[256,384]{1,0:T(8,128)(2,1)S(1)} %copy-done.6, bf16[384,256]{1,0:T(8,128)(2,1)S(1)} %copy.116.dmt_ref, bf16[256,384]{1,0:T(8,128)(2,1)S(1)} %convolution_convert_fusion.14.dm_ref, ...), custom_call_target="tpu_custom_call" | custom-call | flops 17999998976 | bytes 14000000 | tf_op jit(solution)/shard_map/cross_bwd/pallas_call | solution.py:300
  285.2 4.5 collective-permute-start.24
  293.8 7.8 %collective-permute-done.24 = bf16[256,768]{1,0:T(8,128)(2,1)S(1)} collective-permute-done((bf16[256,768]{1,0:T(8,128)(2,1)S(1)}, bf16[256,768]{1,0:T(8,128)(2,1)S(1)}, u32[]{:S(2)}, u32[]{:S(2)}) %collective-permute-start.24) | collective-permute-done | bytes 393248 | tf_op jit(solution)/shard_map/ppermute | solution.py:41
  303.3 2.9 self_bwd.1
  317.4 5.8 %collective-permute-start.89 = (bf16[192,768]{1,0:T(8,128)(2,1)S(1)}, bf16[192,768]{1,0:T(8,128)(2,1)S(1)}, u32[]{:S(2)}, u32[]{:S(2)}) collective-permute-start(bf16[192,768]{1,0:T(8,128)(2,1)S(1)} %bitcast.111), channel_id=1, source_target_pairs={{0,32},{2,34},{4,36},{6,38},{8,40},{10,42},{12,44},{14,46},{16,48}... | collective-permute-start | bytes 884744 | tf_op jit(solution)/shard_map/ppermute | solution.py:37
  323.2 7.5 %collective-permute-done.25 = bf16[256,768]{1,0:T(8,128)(2,1)S(1)} collective-permute-done((bf16[256,768]{1,0:T(8,128)(2,1)S(1)}, bf16[256,768]{1,0:T(8,128)(2,1)S(1)}, u32[]{:S(2)}, u32[]{:S(2)}) %collective-permute-start.25) | collective-permute-done | bytes 393248 | tf_op jit(solution)/shard_map/ppermute | solution.py:41
  333.1 6.8 %collective-permute-start.82 = (bf16[192,768]{1,0:T(8,128)(2,1)S(1)}, bf16[192,768]{1,0:T(8,128)(2,1)S(1)}, u32[]{:S(2)}, u32[]{:S(2)}) collective-permute-start(bf16[192,768]{1,0:T(8,128)(2,1)S(1)} %get-tuple-element.154), channel_id=1, source_target_pairs={{0,192},{2,194},{4,196},{6,198},{8,200},{10,202},{12,204},{14,206}... | collective-permute-start | bytes 884744 | tf_op jit(solution)/shard_map/ppermute | solution.py:37
  342.9 9.9 %collective-permute-done.82 = bf16[192,768]{1,0:T(8,128)(2,1)S(1)} collective-permute-done((bf16[192,768]{1,0:T(8,128)(2,1)S(1)}, bf16[192,768]{1,0:T(8,128)(2,1)S(1)}, u32[]{:S(2)}, u32[]{:S(2)}) %collective-permute-start.82) | collective-permute-done | bytes 294944 | tf_op jit(solution)/shard_map/ppermute | solution.py:37
  352.8 3.7 collective-permute-start.91
  359.2 3.8 collective-permute-start.85
  363.0 4.1 collective-permute-start.86
  382.6 4.3 collective-permute-done.48
  386.9 4.3 collective-permute-start.54
  393.8 7.0 %collective-permute-done.54 = bf16[192,640]{1,0:T(8,128)(2,1)S(1)} collective-permute-done((bf16[192,640]{1,0:T(8,128)(2,1)S(1)}, bf16[192,640]{1,0:T(8,128)(2,1)S(1)}, u32[]{:S(2)}, u32[]{:S(2)}) %collective-permute-start.54) | collective-permute-done | bytes 245792 | tf_op jit(solution)/shard_map/ppermute | solution.py:37
  400.8 3.7 collective-permute-start.51
  406.2 2.9 collective-permute-done.51
  409.1 3.1 collective-permute-start.57
  420.9 3.1 collective-permute-start.60
  441.6 3.5 collective-permute-start.37
  445.1 11.8 %collective-permute-done.27 = bf16[1024,384]{1,0:T(8,128)(2,1)S(1)} collective-permute-done((bf16[1024,384]{1,0:T(8,128)(2,1)S(1)}, bf16[1024,384]{1,0:T(8,128)(2,1)S(1)}, u32[]{:S(2)}, u32[]{:S(2)}) %collective-permute-start.27) | collective-permute-done | bytes 786464 | tf_op jit(solution)/shard_map/ppermute | solution.py:37
  459.3 16.1 %collective-permute-done.29 = bf16[1024,384]{1,0:T(8,128)(2,1)S(1)} collective-permute-done((bf16[1024,384]{1,0:T(8,128)(2,1)S(1)}, bf16[1024,384]{1,0:T(8,128)(2,1)S(1)}, u32[]{:S(2)}, u32[]{:S(2)}) %collective-permute-start.29) | collective-permute-done | bytes 786464 | tf_op jit(solution)/shard_map/ppermute | solution.py:37
  479.4 2.9 collective-permute-done.39
  482.9 4.3 collective-permute-start.40
  490.8 7.0 %collective-permute-start.33 = (bf16[64,384]{1,0:T(8,128)(2,1)S(1)}, bf16[64,384]{1,0:T(8,128)(2,1)S(1)}, u32[]{:S(2)}, u32[]{:S(2)}) collective-permute-start(bf16[64,384]{1,0:T(8,128)(2,1)S(1)} %get-tuple-element.204), channel_id=1, source_target_pairs={{0,12},{2,14},{4,0},{6,2},{8,4},{10,6},{12,8},{14,10},{16,28},{18,... | collective-permute-start | bytes 147464 | tf_op jit(solution)/shard_map/ppermute | solution.py:37
  501.0 4.6 collective-permute-start.43
  522.3 3.1 collective-permute-done.66
  528.8 4.5 collective-permute-start.74
  534.8 3.8 collective-permute-done.75
  545.3 3.6 collective-permute-done.46
  (493 shorter events, 181.1 us)
Async XLA Ops:
  3.0 10.7 %collective-permute-start.2 = (bf16[64,384]{1,0:T(8,128)(2,1)S(1)}, bf16[64,384]{1,0:T(8,128)(2,1)S(1)}, u32[]{:S(2)}, u32[]{:S(2)}) collective-permute-start(bf16[64,384]{1,0:T(8,128)(2,1)S(1)} %get-tuple-element.239), channel_id=1, source_target_pairs={{0,8},{2,10},{4,12},{6,14},{8,0},{10,2},{12,4},{14,6},{16,24},{18,... | collective-permute-start | bytes 147464 | tf_op jit(solution)/shard_map/ppermute | solution.py:37
  9.2 21.0 %collective-permute-start.11 = (bf16[64,384]{1,0:T(8,128)(2,1)S(1)}, bf16[64,384]{1,0:T(8,128)(2,1)S(1)}, u32[]{:S(2)}, u32[]{:S(2)}) collective-permute-start(bf16[64,384]{1,0:T(8,128)(2,1)S(1)} %get-tuple-element.241), channel_id=1, source_target_pairs={{0,4},{2,6},{4,8},{6,10},{8,12},{10,14},{12,0},{14,2},{16,20},{18,... | collective-permute-start | bytes 147464 | tf_op jit(solution)/shard_map/ppermute | solution.py:37
  10.3 19.9 %collective-permute-start.12 = (bf16[64,384]{1,0:T(8,128)(2,1)S(1)}, bf16[64,384]{1,0:T(8,128)(2,1)S(1)}, u32[]{:S(2)}, u32[]{:S(2)}) collective-permute-start(bf16[64,384]{1,0:T(8,128)(2,1)S(1)} %get-tuple-element.241), channel_id=1, source_target_pairs={{0,8},{2,10},{4,12},{6,14},{8,0},{10,2},{12,4},{14,6},{16,24},{18,... | collective-permute-start | bytes 147464 | tf_op jit(solution)/shard_map/ppermute | solution.py:37
  10.8 19.4 %collective-permute-start.13 = (bf16[64,384]{1,0:T(8,128)(2,1)S(1)}, bf16[64,384]{1,0:T(8,128)(2,1)S(1)}, u32[]{:S(2)}, u32[]{:S(2)}) collective-permute-start(bf16[64,384]{1,0:T(8,128)(2,1)S(1)} %get-tuple-element.241), channel_id=1, source_target_pairs={{0,12},{2,14},{4,0},{6,2},{8,4},{10,6},{12,8},{14,10},{16,28},{18,... | collective-permute-start | bytes 147464 | tf_op jit(solution)/shard_map/ppermute | solution.py:37
  29.2 36.5 %collective-permute-start.7 = (bf16[1024,384]{1,0:T(8,128)(2,1)}, bf16[1024,384]{1,0:T(8,128)(2,1)S(1)}, u32[]{:S(2)}, u32[]{:S(2)}) collective-permute-start(bf16[1024,384]{1,0:T(8,128)(2,1)} %get-tuple-element.210), channel_id=1, source_target_pairs={{0,64},{2,66},{4,68},{6,70},{8,72},{10,74},{12,76},{14,78},{16,80}... | collective-permute-start | bytes 2359304 | tf_op jit(solution)/shard_map/ppermute | solution.py:37
  30.3 24.2 %collective-permute-start.14 = (bf16[256,384]{1,0:T(8,128)(2,1)S(1)}, bf16[256,384]{1,0:T(8,128)(2,1)S(1)}, u32[]{:S(2)}, u32[]{:S(2)}) collective-permute-start(bf16[256,384]{1,0:T(8,128)(2,1)S(1)} %pad_maximum_fusion.2), channel_id=1, source_target_pairs={{0,64},{2,66},{4,68},{6,70},{8,72},{10,74},{12,76},{14,78},{16,80}... | collective-permute-start | bytes 589832 | tf_op jit(solution)/shard_map/ppermute | solution.py:37
  31.9 28.3 %collective-permute-start.15 = (bf16[256,384]{1,0:T(8,128)(2,1)S(1)}, bf16[256,384]{1,0:T(8,128)(2,1)S(1)}, u32[]{:S(2)}, u32[]{:S(2)}) collective-permute-start(bf16[256,384]{1,0:T(8,128)(2,1)S(1)} %pad_maximum_fusion.2), channel_id=1, source_target_pairs={{0,128},{2,130},{4,132},{6,134},{8,136},{10,138},{12,140},{14,142}... | collective-permute-start | bytes 589832 | tf_op jit(solution)/shard_map/ppermute | solution.py:37
  34.0 26.9 %collective-permute-start.16 = (bf16[256,384]{1,0:T(8,128)(2,1)S(1)}, bf16[256,384]{1,0:T(8,128)(2,1)S(1)}, u32[]{:S(2)}, u32[]{:S(2)}) collective-permute-start(bf16[256,384]{1,0:T(8,128)(2,1)S(1)} %pad_maximum_fusion.2), channel_id=1, source_target_pairs={{0,192},{2,194},{4,196},{6,198},{8,200},{10,202},{12,204},{14,206}... | collective-permute-start | bytes 589832 | tf_op jit(solution)/shard_map/ppermute | solution.py:37
  37.7 36.5 %collective-permute-start.8 = (bf16[1024,384]{1,0:T(8,128)(2,1)}, bf16[1024,384]{1,0:T(8,128)(2,1)}, u32[]{:S(2)}, u32[]{:S(2)}) collective-permute-start(bf16[1024,384]{1,0:T(8,128)(2,1)} %get-tuple-element.210), channel_id=1, source_target_pairs={{0,128},{2,130},{4,132},{6,134},{8,136},{10,138},{12,140},{14,142}... | collective-permute-start | bytes 2359304 | tf_op jit(solution)/shard_map/ppermute | solution.py:37
  54.5 27.5 %collective-permute-start.9 = (bf16[1024,384]{1,0:T(8,128)(2,1)}, bf16[1024,384]{1,0:T(8,128)(2,1)}, u32[]{:S(2)}, u32[]{:S(2)}) collective-permute-start(bf16[1024,384]{1,0:T(8,128)(2,1)} %get-tuple-element.210), channel_id=1, source_target_pairs={{0,192},{2,194},{4,196},{6,198},{8,200},{10,202},{12,204},{14,206}... | collective-permute-start | bytes 2359304 | tf_op jit(solution)/shard_map/ppermute | solution.py:37
  61.6 22.6 %collective-permute-start.17 = (bf16[4,1,256,384]{3,2,1,0:T(8,128)(2,1)}, bf16[4,1,256,384]{3,2,1,0:T(8,128)(2,1)}, u32[]{:S(2)}, u32[]{:S(2)}) collective-permute-start(bf16[4,1,256,384]{3,2,1,0:T(8,128)(2,1)} %bitcast.2), channel_id=1, source_target_pairs={{0,16},{2,18},{4,20},{6,22},{8,24},{10,26},{12,28},{14,30},{16,32}... | collective-permute-start | bytes 2359304 | tf_op jit(solution)/shard_map/ppermute | solution.py:37
  61.9 27.2 %collective-permute-start.18 = (bf16[4,1,256,384]{3,2,1,0:T(8,128)(2,1)}, bf16[4,1,256,384]{3,2,1,0:T(8,128)(2,1)}, u32[]{:S(2)}, u32[]{:S(2)}) collective-permute-start(bf16[4,1,256,384]{3,2,1,0:T(8,128)(2,1)} %bitcast.2), channel_id=1, source_target_pairs={{0,32},{2,34},{4,36},{6,38},{8,40},{10,42},{12,44},{14,46},{16,48}... | collective-permute-start | bytes 2359304 | tf_op jit(solution)/shard_map/ppermute | solution.py:37
  66.5 22.5 %collective-permute-start.19 = (bf16[4,1,256,384]{3,2,1,0:T(8,128)(2,1)}, bf16[4,1,256,384]{3,2,1,0:T(8,128)(2,1)}, u32[]{:S(2)}, u32[]{:S(2)}) collective-permute-start(bf16[4,1,256,384]{3,2,1,0:T(8,128)(2,1)} %bitcast.2), channel_id=1, source_target_pairs={{0,48},{2,50},{4,52},{6,54},{8,56},{10,58},{12,60},{14,62},{16,0},... | collective-permute-start | bytes 2359304 | tf_op jit(solution)/shard_map/ppermute | solution.py:37
  74.3 61.2 %collective-permute-start = (bf16[256,768]{1,0:T(8,128)(2,1)S(1)}, bf16[256,768]{1,0:T(8,128)(2,1)S(1)}, u32[]{:S(2)}, u32[]{:S(2)}) collective-permute-start(bf16[256,768]{1,0:T(8,128)(2,1)S(1)} %get-tuple-element.42), channel_id=1, source_target_pairs={{0,1},{1,0},{2,3},{3,2},{4,5},{5,4},{6,7},{7,6},{8,9},{9,8},{10,11... | collective-permute-start | bytes 1179656 | tf_op jit(solution)/shard_map/ppermute | solution.py:41
  84.2 69.5 %collective-permute-start.10 = (bf16[4096,384]{1,0:T(8,128)(2,1)}, bf16[4096,384]{1,0:T(8,128)(2,1)}, u32[]{:S(2)}, u32[]{:S(2)}) collective-permute-start(bf16[4096,384]{1,0:T(8,128)(2,1)} %constant_dynamic-update-slice_fusion.7.refs_1_.k_ref), channel_id=1, source_target_pairs={{0,2},{2,0},{4,6},{6,4},{8,10},{10,8},{12,14},{14,12},{16,18},{18,... | collective-permute-start | bytes 9437192 | tf_op jit(solution)/shard_map/ppermute | solution.py:37
  92.3 61.3 %collective-permute-start.20 = (bf16[4096,384]{1,0:T(8,128)(2,1)}, bf16[4096,384]{1,0:T(8,128)(2,1)}, u32[]{:S(2)}, u32[]{:S(2)}) collective-permute-start(bf16[4096,384]{1,0:T(8,128)(2,1)} %bitcast.6.refs_2_.v_ref), channel_id=1, source_target_pairs={{0,2},{2,0},{4,6},{6,4},{8,10},{10,8},{12,14},{14,12},{16,18},{18,... | collective-permute-start | bytes 9437192 | tf_op jit(solution)/shard_map/ppermute | solution.py:37
  171.2 16.7 %collective-permute-start.21 = (bf16[256,768]{1,0:T(8,128)(2,1)S(1)}, bf16[256,768]{1,0:T(8,128)(2,1)S(1)}, u32[]{:S(2)}, u32[]{:S(2)}) collective-permute-start(bf16[256,768]{1,0:T(8,128)(2,1)S(1)} %convolution_convert_fusion.13), channel_id=1, source_target_pairs={{0,1},{1,0},{2,3},{3,2},{4,5},{5,4},{6,7},{7,6},{8,9},{9,8},{10,11... | collective-permute-start | bytes 1179656 | tf_op jit(solution)/shard_map/ppermute | solution.py:41
  190.6 25.3 %collective-permute-start.22 = (bf16[256,768]{1,0:T(8,128)(2,1)S(1)}, bf16[256,768]{1,0:T(8,128)(2,1)S(1)}, u32[]{:S(2)}, u32[]{:S(2)}) collective-permute-start(bf16[256,768]{1,0:T(8,128)(2,1)S(1)} %convolution_convert_fusion.11), channel_id=1, source_target_pairs={{0,1},{1,0},{2,3},{3,2},{4,5},{5,4},{6,7},{7,6},{8,9},{9,8},{10,11... | collective-permute-start | bytes 1179656 | tf_op jit(solution)/shard_map/ppermute | solution.py:41
  220.8 20.8 %collective-permute-start.23 = (bf16[256,768]{1,0:T(8,128)(2,1)}, bf16[256,768]{1,0:T(8,128)(2,1)}, u32[]{:S(2)}, u32[]{:S(2)}) collective-permute-start(bf16[256,768]{1,0:T(8,128)(2,1)} %convolution_convert_fusion.10), channel_id=1, source_target_pairs={{0,1},{1,0},{2,3},{3,2},{4,5},{5,4},{6,7},{7,6},{8,9},{9,8},{10,11... | collective-permute-start | bytes 1179656 | tf_op jit(solution)/shard_map/ppermute | solution.py:41
  285.2 16.3 %collective-permute-start.24 = (bf16[256,768]{1,0:T(8,128)(2,1)S(1)}, bf16[256,768]{1,0:T(8,128)(2,1)S(1)}, u32[]{:S(2)}, u32[]{:S(2)}) collective-permute-start(bf16[256,768]{1,0:T(8,128)(2,1)S(1)} %convolution_convert_fusion.12), channel_id=1, source_target_pairs={{0,1},{1,0},{2,3},{3,2},{4,5},{5,4},{6,7},{7,6},{8,9},{9,8},{10,11... | collective-permute-start | bytes 1179656 | tf_op jit(solution)/shard_map/ppermute | solution.py:41
  293.0 18.7 %collective-permute-start.81 = (bf16[768,1536]{1,0:T(8,128)(2,1)}, bf16[768,1536]{1,0:T(8,128)(2,1)}, u32[]{:S(2)}, u32[]{:S(2)}) collective-permute-start(bf16[768,1536]{1,0:T(8,128)(2,1)} %fusion), channel_id=1, source_target_pairs={{0,2},{2,0},{4,6},{6,4},{8,10},{10,8},{12,14},{14,12},{16,18},{18,... | collective-permute-start | bytes 7077896 | tf_op jit(solution)/shard_map/ppermute | solution.py:37
  293.1 140.4 %collective-permute-start.26 = (bf16[4096,384]{1,0:T(8,128)(2,1)}, bf16[4096,384]{1,0:T(8,128)(2,1)}, u32[]{:S(2)}, u32[]{:S(2)}) collective-permute-start(bf16[4096,384]{1,0:T(8,128)(2,1)} %get-tuple-element.58), channel_id=1, source_target_pairs={{0,2},{2,0},{4,6},{6,4},{8,10},{10,8},{12,14},{14,12},{16,18},{18,... | collective-permute-start | bytes 9437192 | tf_op jit(solution)/shard_map/ppermute | solution.py:37
  308.8 64.2 %collective-permute-start.47 = (bf16[768,1280]{0,1:T(8,128)(2,1)S(1)}, bf16[768,1280]{0,1:T(8,128)(2,1)S(1)}, u32[]{:S(2)}, u32[]{:S(2)}) collective-permute-start(bf16[768,1280]{0,1:T(8,128)(2,1)S(1)} %constant_dynamic-slice_fusion.23), channel_id=1, source_target_pairs={{0,2},{2,0},{4,6},{6,4},{8,10},{10,8},{12,14},{14,12},{16,18},{18,... | collective-permute-start | bytes 5898248 | tf_op jit(solution)/shard_map/ppermute | solution.py:37
  308.9 21.8 %collective-permute-start.25 = (bf16[256,768]{1,0:T(8,128)(2,1)S(1)}, bf16[256,768]{1,0:T(8,128)(2,1)S(1)}, u32[]{:S(2)}, u32[]{:S(2)}) collective-permute-start(bf16[256,768]{1,0:T(8,128)(2,1)S(1)} %get-tuple-element.56), channel_id=1, source_target_pairs={{0,1},{1,0},{2,3},{3,2},{4,5},{5,4},{6,7},{7,6},{8,9},{9,8},{10,11... | collective-permute-start | bytes 1179656 | tf_op jit(solution)/shard_map/ppermute | solution.py:41
  314.9 18.3 %collective-permute-start.88 = (bf16[192,768]{1,0:T(8,128)(2,1)S(1)}, bf16[192,768]{1,0:T(8,128)(2,1)S(1)}, u32[]{:S(2)}, u32[]{:S(2)}) collective-permute-start(bf16[192,768]{1,0:T(8,128)(2,1)S(1)} %bitcast.112), channel_id=1, source_target_pairs={{0,48},{2,50},{4,52},{6,54},{8,56},{10,58},{12,60},{14,62},{16,0},... | collective-permute-start | bytes 884744 | tf_op jit(solution)/shard_map/ppermute | solution.py:37
  317.4 22.6 %collective-permute-start.89 = (bf16[192,768]{1,0:T(8,128)(2,1)S(1)}, bf16[192,768]{1,0:T(8,128)(2,1)S(1)}, u32[]{:S(2)}, u32[]{:S(2)}) collective-permute-start(bf16[192,768]{1,0:T(8,128)(2,1)S(1)} %bitcast.111), channel_id=1, source_target_pairs={{0,32},{2,34},{4,36},{6,38},{8,40},{10,42},{12,44},{14,46},{16,48}... | collective-permute-start | bytes 884744 | tf_op jit(solution)/shard_map/ppermute | solution.py:37
  333.1 19.6 %collective-permute-start.82 = (bf16[192,768]{1,0:T(8,128)(2,1)S(1)}, bf16[192,768]{1,0:T(8,128)(2,1)S(1)}, u32[]{:S(2)}, u32[]{:S(2)}) collective-permute-start(bf16[192,768]{1,0:T(8,128)(2,1)S(1)} %get-tuple-element.154), channel_id=1, source_target_pairs={{0,192},{2,194},{4,196},{6,198},{8,200},{10,202},{12,204},{14,206}... | collective-permute-start | bytes 884744 | tf_op jit(solution)/shard_map/ppermute | solution.py:37
  340.0 16.5 %collective-permute-start.83 = (bf16[192,768]{1,0:T(8,128)(2,1)S(1)}, bf16[192,768]{1,0:T(8,128)(2,1)S(1)}, u32[]{:S(2)}, u32[]{:S(2)}) collective-permute-start(bf16[192,768]{1,0:T(8,128)(2,1)S(1)} %get-tuple-element.156), channel_id=1, source_target_pairs={{0,128},{2,130},{4,132},{6,134},{8,136},{10,138},{12,140},{14,142}... | collective-permute-start | bytes 884744 | tf_op jit(solution)/shard_map/ppermute | solution.py:37
  341.4 15.1 %collective-permute-start.84 = (bf16[192,768]{1,0:T(8,128)(2,1)S(1)}, bf16[192,768]{1,0:T(8,128)(2,1)S(1)}, u32[]{:S(2)}, u32[]{:S(2)}) collective-permute-start(bf16[192,768]{1,0:T(8,128)(2,1)S(1)} %get-tuple-element.155), channel_id=1, source_target_pairs={{0,64},{2,66},{4,68},{6,70},{8,72},{10,74},{12,76},{14,78},{16,80}... | collective-permute-start | bytes 884744 | tf_op jit(solution)/shard_map/ppermute | solution.py:37
  367.2 71.4 %collective-permute-start.36 = (bf16[4096,384]{1,0:T(8,128)(2,1)}, bf16[4096,384]{1,0:T(8,128)(2,1)}, u32[]{:S(2)}, u32[]{:S(2)}) collective-permute-start(bf16[4096,384]{1,0:T(8,128)(2,1)} %get-tuple-element.60), channel_id=1, source_target_pairs={{0,2},{2,0},{4,6},{6,4},{8,10},{10,8},{12,14},{14,12},{16,18},{18,... | collective-permute-start | bytes 9437192 | tf_op jit(solution)/shard_map/ppermute | solution.py:37
  378.2 13.0 %collective-permute-start.49 = (bf16[192,640]{0,1:T(8,128)(2,1)S(1)}, bf16[192,640]{0,1:T(8,128)(2,1)S(1)}, u32[]{:S(2)}, u32[]{:S(2)}) collective-permute-start(bf16[192,640]{0,1:T(8,128)(2,1)S(1)} %get-tuple-element.163), channel_id=1, source_target_pairs={{0,128},{2,130},{4,132},{6,134},{8,136},{10,138},{12,140},{14,142}... | collective-permute-start | bytes 737288 | tf_op jit(solution)/shard_map/ppermute | solution.py:37
  379.8 13.5 %collective-permute-start.50 = (bf16[192,640]{0,1:T(8,128)(2,1)S(1)}, bf16[192,640]{0,1:T(8,128)(2,1)S(1)}, u32[]{:S(2)}, u32[]{:S(2)}) collective-permute-start(bf16[192,640]{0,1:T(8,128)(2,1)S(1)} %get-tuple-element.162), channel_id=1, source_target_pairs={{0,64},{2,66},{4,68},{6,70},{8,72},{10,74},{12,76},{14,78},{16,80}... | collective-permute-start | bytes 737288 | tf_op jit(solution)/shard_map/ppermute | solution.py:37
  386.9 13.9 %collective-permute-start.54 = (bf16[192,640]{1,0:T(8,128)(2,1)S(1)}, bf16[192,640]{1,0:T(8,128)(2,1)S(1)}, u32[]{:S(2)}, u32[]{:S(2)}) collective-permute-start(bf16[192,640]{1,0:T(8,128)(2,1)S(1)} %bitcast.115), channel_id=1, source_target_pairs={{0,48},{2,50},{4,52},{6,54},{8,56},{10,58},{12,60},{14,62},{16,0},... | collective-permute-start | bytes 737288 | tf_op jit(solution)/shard_map/ppermute | solution.py:37
  391.2 13.3 %collective-permute-start.55 = (bf16[192,640]{1,0:T(8,128)(2,1)S(1)}, bf16[192,640]{1,0:T(8,128)(2,1)S(1)}, u32[]{:S(2)}, u32[]{:S(2)}) collective-permute-start(bf16[192,640]{1,0:T(8,128)(2,1)S(1)} %bitcast.114), channel_id=1, source_target_pairs={{0,32},{2,34},{4,36},{6,38},{8,40},{10,42},{12,44},{14,46},{16,48}... | collective-permute-start | bytes 737288 | tf_op jit(solution)/shard_map/ppermute | solution.py:37
  393.3 12.0 %collective-permute-start.56 = (bf16[192,640]{1,0:T(8,128)(2,1)S(1)}, bf16[192,640]{1,0:T(8,128)(2,1)S(1)}, u32[]{:S(2)}, u32[]{:S(2)}) collective-permute-start(bf16[192,640]{1,0:T(8,128)(2,1)S(1)} %bitcast.113), channel_id=1, source_target_pairs={{0,16},{2,18},{4,20},{6,22},{8,24},{10,26},{12,28},{14,30},{16,32}... | collective-permute-start | bytes 737288 | tf_op jit(solution)/shard_map/ppermute | solution.py:37
  436.4 20.4 %collective-permute-start.27 = (bf16[1024,384]{1,0:T(8,128)(2,1)S(1)}, bf16[1024,384]{1,0:T(8,128)(2,1)S(1)}, u32[]{:S(2)}, u32[]{:S(2)}) collective-permute-start(bf16[1024,384]{1,0:T(8,128)(2,1)S(1)} %get-tuple-element.139), channel_id=1, source_target_pairs={{0,192},{2,194},{4,196},{6,198},{8,200},{10,202},{12,204},{14,206}... | collective-permute-start | bytes 2359304 | tf_op jit(solution)/shard_map/ppermute | solution.py:37
  437.3 21.9 %collective-permute-start.28 = (bf16[1024,384]{1,0:T(8,128)(2,1)S(1)}, bf16[1024,384]{1,0:T(8,128)(2,1)S(1)}, u32[]{:S(2)}, u32[]{:S(2)}) collective-permute-start(bf16[1024,384]{1,0:T(8,128)(2,1)S(1)} %get-tuple-element.141), channel_id=1, source_target_pairs={{0,128},{2,130},{4,132},{6,134},{8,136},{10,138},{12,140},{14,142}... | collective-permute-start | bytes 2359304 | tf_op jit(solution)/shard_map/ppermute | solution.py:37
  438.6 36.8 %collective-permute-start.29 = (bf16[1024,384]{1,0:T(8,128)(2,1)S(1)}, bf16[1024,384]{1,0:T(8,128)(2,1)S(1)}, u32[]{:S(2)}, u32[]{:S(2)}) collective-permute-start(bf16[1024,384]{1,0:T(8,128)(2,1)S(1)} %get-tuple-element.140), channel_id=1, source_target_pairs={{0,64},{2,66},{4,68},{6,70},{8,72},{10,74},{12,76},{14,78},{16,80}... | collective-permute-start | bytes 2359304 | tf_op jit(solution)/shard_map/ppermute | solution.py:37
  441.6 36.9 %collective-permute-start.37 = (bf16[1024,384]{1,0:T(8,128)(2,1)S(1)}, bf16[1024,384]{1,0:T(8,128)(2,1)S(1)}, u32[]{:S(2)}, u32[]{:S(2)}) collective-permute-start(bf16[1024,384]{1,0:T(8,128)(2,1)S(1)} %bitcast.109), channel_id=1, source_target_pairs={{0,48},{2,50},{4,52},{6,54},{8,56},{10,58},{12,60},{14,62},{16,0},... | collective-permute-start | bytes 2359304 | tf_op jit(solution)/shard_map/ppermute | solution.py:37
  445.1 34.4 %collective-permute-start.38 = (bf16[1024,384]{1,0:T(8,128)(2,1)S(1)}, bf16[1024,384]{1,0:T(8,128)(2,1)S(1)}, u32[]{:S(2)}, u32[]{:S(2)}) collective-permute-start(bf16[1024,384]{1,0:T(8,128)(2,1)S(1)} %bitcast.108), channel_id=1, source_target_pairs={{0,32},{2,34},{4,36},{6,38},{8,40},{10,42},{12,44},{14,46},{16,48}... | collective-permute-start | bytes 2359304 | tf_op jit(solution)/shard_map/ppermute | solution.py:37
  456.9 25.5 %collective-permute-start.39 = (bf16[1024,384]{1,0:T(8,128)(2,1)S(1)}, bf16[1024,384]{1,0:T(8,128)(2,1)S(1)}, u32[]{:S(2)}, u32[]{:S(2)}) collective-permute-start(bf16[1024,384]{1,0:T(8,128)(2,1)S(1)} %bitcast.107), channel_id=1, source_target_pairs={{0,16},{2,18},{4,20},{6,22},{8,24},{10,26},{12,28},{14,30},{16,32}... | collective-permute-start | bytes 2359304 | tf_op jit(solution)/shard_map/ppermute | solution.py:37
  475.8 12.4 %collective-permute-start.30 = (bf16[256,384]{1,0:T(8,128)(2,1)S(1)}, bf16[256,384]{1,0:T(8,128)(2,1)S(1)}, u32[]{:S(2)}, u32[]{:S(2)}) collective-permute-start(bf16[256,384]{1,0:T(8,128)(2,1)S(1)} %get-tuple-element.165), channel_id=1, source_target_pairs={{0,48},{2,50},{4,52},{6,54},{8,56},{10,58},{12,60},{14,62},{16,0},... | collective-permute-start | bytes 589832 | tf_op jit(solution)/shard_map/ppermute | solution.py:37
  478.5 10.8 %collective-permute-start.31 = (bf16[256,384]{1,0:T(8,128)(2,1)S(1)}, bf16[256,384]{1,0:T(8,128)(2,1)S(1)}, u32[]{:S(2)}, u32[]{:S(2)}) collective-permute-start(bf16[256,384]{1,0:T(8,128)(2,1)S(1)} %get-tuple-element.167), channel_id=1, source_target_pairs={{0,32},{2,34},{4,36},{6,38},{8,40},{10,42},{12,44},{14,46},{16,48}... | collective-permute-start | bytes 589832 | tf_op jit(solution)/shard_map/ppermute | solution.py:37
  478.5 12.1 %collective-permute-start.32 = (bf16[256,384]{1,0:T(8,128)(2,1)S(1)}, bf16[256,384]{1,0:T(8,128)(2,1)S(1)}, u32[]{:S(2)}, u32[]{:S(2)}) collective-permute-start(bf16[256,384]{1,0:T(8,128)(2,1)S(1)} %get-tuple-element.166), channel_id=1, source_target_pairs={{0,16},{2,18},{4,20},{6,22},{8,24},{10,26},{12,28},{14,30},{16,32}... | collective-permute-start | bytes 589832 | tf_op jit(solution)/shard_map/ppermute | solution.py:37
  482.9 15.5 %collective-permute-start.40 = (bf16[256,384]{1,0:T(8,128)(2,1)S(1)}, bf16[256,384]{1,0:T(8,128)(2,1)S(1)}, u32[]{:S(2)}, u32[]{:S(2)}) collective-permute-start(bf16[256,384]{1,0:T(8,128)(2,1)S(1)} %get-tuple-element.168), channel_id=1, source_target_pairs={{0,192},{2,194},{4,196},{6,198},{8,200},{10,202},{12,204},{14,206}... | collective-permute-start | bytes 589832 | tf_op jit(solution)/shard_map/ppermute | solution.py:37
  487.2 13.7 %collective-permute-start.41 = (bf16[256,384]{1,0:T(8,128)(2,1)S(1)}, bf16[256,384]{1,0:T(8,128)(2,1)S(1)}, u32[]{:S(2)}, u32[]{:S(2)}) collective-permute-start(bf16[256,384]{1,0:T(8,128)(2,1)S(1)} %get-tuple-element.170), channel_id=1, source_target_pairs={{0,128},{2,130},{4,132},{6,134},{8,136},{10,138},{12,140},{14,142}... | collective-permute-start | bytes 589832 | tf_op jit(solution)/shard_map/ppermute | solution.py:37
  488.2 12.7 %collective-permute-start.42 = (bf16[256,384]{1,0:T(8,128)(2,1)S(1)}, bf16[256,384]{1,0:T(8,128)(2,1)S(1)}, u32[]{:S(2)}, u32[]{:S(2)}) collective-permute-start(bf16[256,384]{1,0:T(8,128)(2,1)S(1)} %get-tuple-element.169), channel_id=1, source_target_pairs={{0,64},{2,66},{4,68},{6,70},{8,72},{10,74},{12,76},{14,78},{16,80}... | collective-permute-start | bytes 589832 | tf_op jit(solution)/shard_map/ppermute | solution.py:37
  490.8 15.5 %collective-permute-start.33 = (bf16[64,384]{1,0:T(8,128)(2,1)S(1)}, bf16[64,384]{1,0:T(8,128)(2,1)S(1)}, u32[]{:S(2)}, u32[]{:S(2)}) collective-permute-start(bf16[64,384]{1,0:T(8,128)(2,1)S(1)} %get-tuple-element.204), channel_id=1, source_target_pairs={{0,12},{2,14},{4,0},{6,2},{8,4},{10,6},{12,8},{14,10},{16,28},{18,... | collective-permute-start | bytes 147464 | tf_op jit(solution)/shard_map/ppermute | solution.py:37
  (145 other events, 1889.0 us)
